TPU v7x, 32 devices: a whole 2x2x4 slice. The times are simulated.
32 devices in a mesh: wide: 8 (over z, y), tp: 4 (over x, core).
Axes of the slice: x: 2, y: 2, z: 4, core: 2. Of those that a mesh axis runs over, the one named last changes fastest.
Arguments:
- tokens: bfloat16 [12800, 768], P(('wide', 'tp')), may hold values from -6 to 6
- norm_gains: bfloat16 [2, 768], P(None, ('wide', 'tp')), may hold values from 0.5 to 1.5
- shifts: bfloat16 [5, 768], P(None, ('wide', 'tp')), may hold values from -1 to 1
- attn_weight: bfloat16 [3, 768, 768], P(None, 'wide', 'tp'), may hold values from -0.3125 to 0.3125
- out_weight: bfloat16 [768, 768], P('tp', 'wide'), may hold values from -0.625 to 0.625
- router_weight: bfloat16 [8, 768], P(None, ('wide', 'tp')), may hold values from -0.15625 to 0.15625
- expert_in: bfloat16 [8, 768, 3072], P('wide', None, 'tp'), may hold values from -0.21875 to 0.21875
- expert_in_bias: bfloat16 [8, 3072], P('wide', 'tp'), may hold values from -1 to 1
- expert_down: bfloat16 [8, 768, 3072], P('wide', None, 'tp'), may hold values from -0.21875 to 0.21875
- expert_down_bias: bfloat16 [8, 768], P('wide', 'tp'), may hold values from -1 to 1
- routes: int32 [12800, 2], P('wide'), may hold values from 0 to 7, all different within a row; in each aligned block of 1600 rows (0 to 1599, 1600 to 3199, ...) at most 504 rows name the same one
- cotangent: bfloat16 [12800, 768], P(('wide', 'tp')), may hold values from -6 to 6
Outputs:
- activations: bfloat16 [12800, 768], P(('wide', 'tp'))
- tokens_grad: float32 [12800, 768], P(('wide', 'tp'))
- norm_gains_grad: float32 [2, 768], P(None, ('wide', 'tp'))
- shifts_grad: float32 [5, 768], P(None, ('wide', 'tp'))
- attn_weight_grad: float32 [3, 768, 768], P(None, 'wide', 'tp')
- out_weight_grad: float32 [768, 768], P('tp', 'wide')
- router_grad: float32 [8, 768], P(None, ('wide', 'tp'))
- expert_in_grad: float32 [8, 768, 3072], P('wide', None, 'tp')
- expert_in_bias_grad: float32 [8, 3072], P('wide', 'tp')
- expert_down_grad: float32 [8, 768, 3072], P('wide', None, 'tp')
- expert_down_bias_grad: float32 [8, 768], P('wide', 'tp')
Inputs may be any that keep to these rules, and one draw needn't show every extreme that they name: `routes`: in each group of 1600 consecutive rows (one index of wide) no expert is named by more than 504 rows, a bound that some block reaches; the two experts of a row differ.
All inputs are finite; a program needn't handle non-finite values.
Results may differ from a plain program's by a relative error of at most 0.028.
Values may be sent and summed in bfloat16 or wider, within the bound.
No kernel may reach another device: no remote copies, remote signals or barrier semaphores. Data moves between devices by JAX's collectives and lax.ppermute only.
A program may use at most 192 MiB of HBM per device.

v0:
```python
import jax
import jax.numpy as jnp
from jax import lax
from jax.sharding import PartitionSpec as P

D = 768
HD = 64
SEQ = 200
BLOCK_IMG = 4
VALID = 197


EPSILON = 1e-06
MASKED = -1000000000.0


def exact_gelu(inputs):
    return jax.nn.gelu(inputs, approximate=False)


def normalize(inputs, gain, shift):
    average = jnp.mean(inputs, axis=-1, keepdims=True)
    centered = inputs - average
    inverse = lax.rsqrt(jnp.mean(centered * centered, axis=-1, keepdims=True) + EPSILON)
    scaled = centered * inverse
    return (scaled * gain + shift, scaled, inverse)


def norm_back(upstream, scaled, inverse, gain):
    grad_hat = upstream * gain
    mean_grad = jnp.mean(grad_hat, axis=-1, keepdims=True)
    mean_cross = jnp.mean(grad_hat * scaled, axis=-1, keepdims=True)
    return inverse * (grad_hat - mean_grad - scaled * mean_cross)


def slot_tables(routes, weight, experts, capacity):
    flattened = routes.reshape(-1)
    onehot = (flattened[:, None] == jnp.arange(experts, dtype=jnp.int32)[None, :]).astype(jnp.int32)
    before = jnp.cumsum(onehot, axis=0, dtype=jnp.int32) - onehot
    places = flattened * capacity + jnp.sum(before * onehot, axis=1, dtype=jnp.int32)
    owners = jnp.arange(flattened.shape[0], dtype=jnp.int32) // 2
    slot_token = jnp.zeros((experts * capacity,), jnp.int32).at[places].set(owners)
    slot_weight = jnp.zeros((experts * capacity,), jnp.float32).at[places].set(weight.reshape(-1))
    return (places, slot_token, slot_weight)


def masked_scores(queries, key_rows):
    scores = jnp.einsum(
        "bqhd,bkhd->bhqk", queries, key_rows, preferred_element_type=jnp.float32
    ) * HD ** (-0.5)
    key_valid = jnp.arange(scores.shape[-1]) < VALID
    return jnp.where(key_valid, scores, MASKED)


def attend_block(block):
    scores = masked_scores(block[0], block[1])
    row_max = jnp.max(scores, axis=-1, keepdims=True)
    exponent = jnp.exp(scores - row_max)
    row_sum = jnp.sum(exponent, axis=-1, keepdims=True)
    attention = (exponent / row_sum).astype(jnp.bfloat16)
    mixed_heads = jnp.einsum(
        "bhqk,bkhd->bqhd", attention, block[2], preferred_element_type=jnp.float32
    )
    return (mixed_heads.astype(jnp.bfloat16), row_max + jnp.log(row_sum))


def attend_back(inputs):
    block, upstream, log_sums = inputs
    scale = HD ** (-0.5)
    attention = jnp.exp(masked_scores(block[0], block[1]) - log_sums)
    grad_attn = jnp.einsum(
        "bqhd,bkhd->bhqk", upstream, block[2], preferred_element_type=jnp.float32
    )
    inner = jnp.sum(attention * grad_attn, axis=-1, keepdims=True)
    grad_scores = (attention * (grad_attn - inner)).astype(jnp.bfloat16)
    grad_query = (
        jnp.einsum("bhqk,bkhd->bqhd", grad_scores, block[1], preferred_element_type=jnp.float32)
        * scale
    )
    grad_key = (
        jnp.einsum("bhqk,bqhd->bkhd", grad_scores, block[0], preferred_element_type=jnp.float32)
        * scale
    )
    grad_value = jnp.einsum(
        "bhqk,bqhd->bkhd",
        attention.astype(jnp.bfloat16),
        upstream,
        preferred_element_type=jnp.float32,
    )
    return jnp.stack([grad_query, grad_key, grad_value])


def body(
    tokens,
    norm_gains,
    shifts,
    attn_weight,
    out_weight,
    router_weight,
    expert_in,
    expert_in_bias,
    expert_down,
    expert_down_bias,
    routes,
    cotangent,
):
    gain_all, shift_all, router_all = (
        lax.all_gather(norm_gains, ("wide", "tp"), axis=1, tiled=True),
        lax.all_gather(shifts, ("wide", "tp"), axis=1, tiled=True),
        lax.all_gather(router_weight, ("wide", "tp"), axis=1, tiled=True),
    )
    gain_all = gain_all.astype(jnp.float32)
    shift_all = shift_all.astype(jnp.float32)
    input_proj, output_proj = (
        lax.all_gather(attn_weight, "wide", axis=1, tiled=True),
        lax.all_gather(out_weight, "wide", axis=1, tiled=True),
    )
    tp_rank = lax.axis_index("tp")
    local_rows = tokens.shape[0]
    group_rows = routes.shape[0]
    width_local = output_proj.shape[0]
    heads_local = width_local // HD
    hidden_local = expert_in.shape[2]
    experts = router_all.shape[0]
    capacity = (10 * group_rows // (4 * experts) + 7) // 8 * 8
    first_row = tp_rank * local_rows
    col_start = tp_rank * width_local
    is_valid = (jnp.arange(group_rows) % SEQ < VALID).astype(jnp.float32)

    def to_group(rows_local):
        return lax.all_gather(rows_local, "tp", axis=0, tiled=True)

    def from_group(partial_rows):
        return lax.psum_scatter(
            partial_rows.astype(jnp.bfloat16), "tp", scatter_dimension=0, tiled=True
        ).astype(jnp.float32)

    inputs_float = tokens.astype(jnp.float32)
    normed, scaled_one, inverse_one = normalize(inputs_float, gain_all[0], shift_all[0])
    normed_group = to_group(normed.astype(jnp.bfloat16))
    bias_pair = lax.dynamic_slice_in_dim(shift_all[1:3], col_start, width_local, 1)
    bias_three = jnp.stack([bias_pair[0], jnp.zeros_like(bias_pair[0]), bias_pair[1]])
    projected = jnp.einsum(
        "td,sde->ste", normed_group, input_proj, preferred_element_type=jnp.float32
    )
    projected_low = (projected + bias_three[:, None, :]).astype(jnp.bfloat16)
    block_count = group_rows // (BLOCK_IMG * SEQ)
    blocks = projected_low.reshape(3, block_count, BLOCK_IMG, SEQ, heads_local, HD).transpose(
        1, 0, 2, 3, 4, 5
    )
    mixed_blocks, log_sums = lax.map(attend_block, blocks)
    mixed_heads = mixed_blocks.reshape(group_rows, width_local)
    attention_sum = from_group(
        jnp.dot(mixed_heads, output_proj, preferred_element_type=jnp.float32)
    )
    residual = inputs_float + attention_sum + shift_all[3]
    normed_two, scaled_two, inverse_two = normalize(residual, gain_all[1], shift_all[4])
    normed_two_low = normed_two.astype(jnp.bfloat16)
    expert_inputs = to_group(normed_two_low)
    logits = jnp.dot(expert_inputs, router_all.T, preferred_element_type=jnp.float32)
    chosen = jnp.take_along_axis(logits, routes, axis=1)
    gate_values = jax.nn.softmax(chosen, axis=1)
    weight = gate_values * is_valid[:, None]
    places, slot_token, slot_weight = slot_tables(routes, weight, experts, capacity)
    rows_all = jnp.take(expert_inputs, slot_token, axis=0).reshape(experts, capacity, D)
    owned_rows = lax.all_to_all(rows_all, "wide", split_axis=0, concat_axis=1, tiled=True)
    pre_act = (
        jnp.einsum("ecd,edf->ecf", owned_rows, expert_in, preferred_element_type=jnp.float32)
        + expert_in_bias.astype(jnp.float32)[:, None, :]
    )
    owned_hidden = exact_gelu(pre_act).astype(jnp.bfloat16)
    owned_result = (
        jnp.einsum("ecf,edf->ecd", owned_hidden, expert_down, preferred_element_type=jnp.float32)
        + lax.dynamic_update_slice(
            jnp.zeros((expert_down_bias.shape[0], D), jnp.float32),
            expert_down_bias.astype(jnp.float32),
            (0, col_start),
        )[:, None, :]
    )
    result_back = (
        lax.all_to_all(
            owned_result.astype(jnp.bfloat16), "wide", split_axis=1, concat_axis=0, tiled=True
        )
        .astype(owned_result.dtype)
        .reshape(experts * capacity, D)
    )
    expert_partial = (
        jnp.zeros((group_rows, D), jnp.float32)
        .at[slot_token]
        .add(slot_weight[:, None] * result_back)
    )
    expert_total = from_group(expert_partial)
    output = (residual + expert_total).astype(jnp.bfloat16)
    grad_out = cotangent.astype(jnp.float32)
    grad_group = to_group(cotangent)
    upstream_all = jnp.take(grad_group, slot_token, axis=0).astype(jnp.float32)
    slot_grads_all = (
        (slot_weight[:, None] * upstream_all).astype(jnp.bfloat16).reshape(experts, capacity, D)
    )
    own_start = lax.axis_index("wide") * expert_in.shape[0]
    grad_slots = jnp.sum(upstream_all * result_back, axis=1)
    owned_grads = lax.all_to_all(slot_grads_all, "wide", split_axis=0, concat_axis=1, tiled=True)
    owned_grad_hidden = jnp.einsum(
        "ecd,edf->ecf", owned_grads, expert_down, preferred_element_type=jnp.float32
    )
    owned_grad_pre = jax.vjp(exact_gelu, pre_act)[1](owned_grad_hidden)[0].astype(jnp.bfloat16)
    owned_grad_in = jnp.einsum(
        "ecf,edf->ecd", owned_grad_pre, expert_in, preferred_element_type=jnp.float32
    )
    grad_in_back = (
        lax.all_to_all(
            owned_grad_in.astype(jnp.bfloat16), "wide", split_axis=1, concat_axis=0, tiled=True
        )
        .astype(owned_grad_in.dtype)
        .reshape(experts * capacity, D)
    )
    grad_rows = jnp.zeros((group_rows, D), jnp.float32).at[slot_token].add(grad_in_back)
    grad_first = jnp.einsum(
        "ecd,ecf->edf", owned_rows, owned_grad_pre, preferred_element_type=jnp.float32
    )
    grad_second = jnp.einsum(
        "ecd,ecf->edf", owned_grads, owned_hidden, preferred_element_type=jnp.float32
    )
    own_first_bias = jnp.sum(owned_grad_pre.astype(jnp.float32), axis=1)
    own_second_bias = lax.dynamic_slice_in_dim(
        jnp.sum(owned_grads.astype(jnp.float32), axis=1), col_start, width_local, 1
    )
    bias_first = lax.dynamic_update_slice_in_dim(
        jnp.zeros((experts, hidden_local), jnp.float32), own_first_bias, own_start, 0
    )
    bias_second = lax.dynamic_update_slice_in_dim(
        jnp.zeros((experts, width_local), jnp.float32), own_second_bias, own_start, 0
    )
    grad_weight = jnp.take(grad_slots, places, axis=0).reshape(group_rows, 2)
    grad_two, grad_weight_local = (
        lax.psum_scatter(
            grad_rows.astype(jnp.bfloat16), "tp", scatter_dimension=0, tiled=True
        ).astype(jnp.float32),
        lax.psum_scatter(
            grad_weight.astype(jnp.bfloat16), "tp", scatter_dimension=0, tiled=True
        ).astype(jnp.float32),
    )
    valid_here = lax.dynamic_slice_in_dim(is_valid, first_row, local_rows, 0)
    gates_here = lax.dynamic_slice_in_dim(gate_values, first_row, local_rows, 0)
    routes_here = lax.dynamic_slice_in_dim(routes, first_row, local_rows, 0)
    grad_gate = grad_weight_local * valid_here[:, None]
    grad_chosen = gates_here * (grad_gate - jnp.sum(gates_here * grad_gate, axis=1, keepdims=True))
    matches = (
        routes_here[:, :, None] == jnp.arange(experts, dtype=jnp.int32)[None, None, :]
    ).astype(jnp.float32)
    grad_logits = jnp.sum(grad_chosen[:, :, None] * matches, axis=1).astype(jnp.bfloat16)
    grad_router = jnp.dot(grad_logits.T, normed_two_low, preferred_element_type=jnp.float32)
    grad_two = grad_two + jnp.dot(grad_logits, router_all, preferred_element_type=jnp.float32)
    grad_gain_two = jnp.sum(grad_two * scaled_two, axis=0)
    grad_shift_two = jnp.sum(grad_two, axis=0)
    grad_mid = grad_out + norm_back(grad_two, scaled_two, inverse_two, gain_all[1])
    grad_out_bias = jnp.sum(grad_mid, axis=0)
    branch_group = to_group(grad_mid.astype(jnp.bfloat16))
    grad_mixed = jnp.dot(branch_group, output_proj.T, preferred_element_type=jnp.float32).astype(
        jnp.bfloat16
    )
    grad_output_proj = jnp.dot(mixed_heads.T, branch_group, preferred_element_type=jnp.float32)
    upstream_blocks = grad_mixed.reshape(block_count, BLOCK_IMG, SEQ, heads_local, HD)
    grad_blocks = lax.map(attend_back, (blocks, upstream_blocks, log_sums))
    grad_proj_in = (
        grad_blocks.transpose(1, 0, 2, 3, 4, 5)
        .reshape(3, group_rows, width_local)
        .astype(jnp.bfloat16)
    )
    grad_input_proj = jnp.einsum(
        "td,ste->sde", normed_group, grad_proj_in, preferred_element_type=jnp.float32
    )
    grad_one = from_group(
        jnp.einsum("ste,sde->td", grad_proj_in, input_proj, preferred_element_type=jnp.float32)
    )
    bias_sums = jnp.sum(grad_proj_in.astype(jnp.float32), axis=1)
    grad_pair = lax.dynamic_update_slice(
        jnp.zeros((2, D), jnp.float32), jnp.stack([bias_sums[0], bias_sums[2]]), (0, col_start)
    )
    grad_gain_one = jnp.sum(grad_one * scaled_one, axis=0)
    grad_shift_one = jnp.sum(grad_one, axis=0)
    grad_input = grad_mid + norm_back(grad_one, scaled_one, inverse_one, gain_all[0])
    grad_in_w, grad_out_w, grad_first_bias, grad_second_bias = (
        lax.psum_scatter(
            grad_input_proj.astype(jnp.bfloat16), "wide", scatter_dimension=1, tiled=True
        ).astype(jnp.float32),
        lax.psum_scatter(
            grad_output_proj.astype(jnp.bfloat16), "wide", scatter_dimension=1, tiled=True
        ).astype(jnp.float32),
        lax.psum_scatter(
            bias_first.T.astype(jnp.bfloat16), "wide", scatter_dimension=1, tiled=True
        ).astype(jnp.float32),
        lax.psum_scatter(
            bias_second.T.astype(jnp.bfloat16), "wide", scatter_dimension=1, tiled=True
        ).astype(jnp.float32),
    )
    grad_gains, grad_shifts, grad_router_w = (
        lax.psum_scatter(
            jnp.stack([grad_gain_one, grad_gain_two]),
            ("wide", "tp"),
            scatter_dimension=1,
            tiled=True,
        ),
        lax.psum_scatter(
            jnp.stack([grad_shift_one, grad_pair[0], grad_pair[1], grad_out_bias, grad_shift_two]),
            ("wide", "tp"),
            scatter_dimension=1,
            tiled=True,
        ),
        lax.psum_scatter(grad_router, ("wide", "tp"), scatter_dimension=1, tiled=True),
    )
    return (
        output,
        grad_input,
        grad_gains,
        grad_shifts,
        grad_in_w,
        grad_out_w,
        grad_router_w,
        grad_first,
        grad_first_bias.T,
        grad_second,
        grad_second_bias.T,
    )


def solution(mesh):
    return jax.shard_map(
        body,
        mesh=mesh,
        in_specs=(
            P(("wide", "tp"), None),
            P(None, ("wide", "tp")),
            P(None, ("wide", "tp")),
            P(None, "wide", "tp"),
            P("tp", "wide"),
            P(None, ("wide", "tp")),
            P("wide", None, "tp"),
            P("wide", "tp"),
            P("wide", None, "tp"),
            P("wide", "tp"),
            P("wide", None),
            P(("wide", "tp"), None),
        ),
        out_specs=(
            P(("wide", "tp"), None),
            P(("wide", "tp"), None),
            P(None, ("wide", "tp")),
            P(None, ("wide", "tp")),
            P(None, "wide", "tp"),
            P("tp", "wide"),
            P(None, ("wide", "tp")),
            P("wide", None, "tp"),
            P("wide", "tp"),
            P("wide", None, "tp"),
            P("wide", "tp"),
        ),
        check_vma=False,
    )
```

profile of v0, /device:TPU:0, one launch (start us, length us, event | category | flops | bytes accessed | tf_op | source)
XLA Modules:
  0.0 1587.6 jit_solution(4187633259624914439)
XLA Ops:
  7.2 43.8 %all-gather.1 = bf16[32,24,5]{1,2,0:T(8,128)(2,1)S(1)} all-gather(bf16[1,24,5]{1,2,0:T(8,128)(2,1)} %bitcast.295), channel_id=1, replica_groups=mesh['wide'=8,'tp'=4] {'wide','tp'}, dimensions={0}, use_global_device_ids=true | all-gather | bytes 7920 | tf_op jit(solution)/shard_map/all_gather | solution.py:109
  54.6 36.6 %all-gather = bf16[32,24,2]{1,2,0:T(2,128)(2,1)S(1)} all-gather(bf16[1,24,2]{1,2,0:T(2,128)(2,1)} %bitcast.297), channel_id=1, replica_groups=mesh['wide'=8,'tp'=4] {'wide','tp'}, dimensions={0}, use_global_device_ids=true | all-gather | bytes 3168 | tf_op jit(solution)/shard_map/all_gather | solution.py:108
  95.2 37.1 %all_gather.30 = bf16[3,768,192]{2,0,1:T(4,128)(2,1)S(1)} all-gather(bf16[3,96,192]{2,0,1:T(4,128)(2,1)S(1)} %copy.153), channel_id=1, replica_groups=mesh['wide'=8,'tp'=4] {'wide'}, dimensions={1}, use_global_device_ids=true | all-gather | bytes 995328 | tf_op jit(solution)/shard_map/all_gather | solution.py:115
  134.5 33.0 %all_gather.31 = bf16[192,768]{0,1:T(8,128)(2,1)} all-gather(bf16[192,96]{0,1:T(8,128)(2,1)S(1)} %copy.157), channel_id=1, replica_groups=mesh['wide'=8,'tp'=4] {'wide'}, dimensions={1}, use_global_device_ids=true | all-gather | bytes 331776 | tf_op jit(solution)/shard_map/all_gather | solution.py:116
  167.6 3.7 fusion.101
  171.6 4.6 reshape.373
  178.5 17.6 %while.22 = (s32[]{:T(128)}, bf16[2,4,200,3,64]{2,1,0,4,3:T(4,128)(2,1)}, f32[2,4,3,200,1]{3,2,1,4,0:T(4,128)}, bf16[2,3,4,200,3,64]{3,5,4,2,1,0:T(8,128)(2,1)S(1)}, s32[]{:T(128)}, /*index=5*/s32[]{:T(128)}, s32[]{}, s32[]{}) while((s32[]{:T(128)}, bf16[2,4,200,3,64]{2,1,0,4,3:T(4,128)(2,1)}, f32[2,4,3,200,1]{3,2,1,4,0:T(4,128)}, ...), condition=%wide.region_5.6_spmd, body=%wide.region_2.5_spmd.sunk | while | flops 128791400 | bytes 15760197 | solution.py:151
  196.1 3.5 reshape.374
  199.6 3.5 convolution_convert_fusion.2
  203.5 33.0 %reduce-scatter.17.cloned.1.call-done = bf16[400,768]{1,0:T(8,128)(2,1)} async-done(((bf16[1600,768]{1,0:T(8,128)(2,1)}), bf16[400,768]{1,0:T(8,128)(2,1)}) %reduce-scatter.17.cloned.1.call-update) | async-done | bytes 614416 | tf_op jit(solution)/shard_map/reduce_scatter | solution.py:134
  246.9 15.8 scatter_custom_fusion
  262.8 2.6 all-gather.10.cloned.1.call-done
  265.4 21.0 %gather_fusion.2 = bf16[4032,768]{1,0:T(8,128)(2,1)} fusion(bf16[1600,768]{1,0:T(8,128)(2,1)} %all-gather.10.cloned.1.call-done, s32[4096]{0:T(1024)S(1)} %pad_clamp_fusion.1), kind=kCustom, calls=%fused_computation.clone | custom fusion | bytes 12402432 | tf_op jit(solution)/shard_map/jit(_take)/gather | solution.py:165
  286.4 7.4 broadcast_select_fusion.1
  293.8 6.0 all-to-all-start
  300.1 136.1 %all-to-all-done = bf16[8,504,768]{2,1,0:T(8,128)(2,1)} async-done(((bf16[8,504,768]{2,1,0:T(8,128)(2,1)}), bf16[8,504,768]{2,1,0:T(8,128)(2,1)}, u32[]{:S(2)}, u32[]{:S(2)}) %all-to-all-start) | async-done | bytes 6193184 | tf_op jit(solution)/shard_map/all_to_all | solution.py:166
  436.2 33.2 %multiply_convert_fusion.1 = (bf16[4032,768]{1,0:T(8,128)(2,1)S(1)}, f32[4032,768]{1,0:T(8,128)}, f32[4032,768]{1,0:T(8,128)}) fusion(f32[768]{0:T(1024)S(1)} %convert_reduce_fusion.5, bf16[4032,768]{1,0:T(8,128)(2,1)} %bitcast.34, bf16[1,768,768]{2,1,0:T(8,128)(2,1)S(1)} %copy-done), kind=kOutput, calls=%fused_computation.63 | convolution fusion | flops 4960714752 | bytes 38341632 | tf_op jit(solution)/shard_map/ecd,edf->ecf/dot_general | solution.py:168
  469.5 5.3 fusion.28
  474.7 45.7 %copy.214 = bf16[1,4032,768]{2,0,1:T(2,128)(2,1)} copy(bf16[1,4032,768]{2,1,0:T(8,128)(2,1)S(1)} %fusion.28) | data formatting | bytes 12386304 | tf_op jit(solution)/shard_map/convert_element_type | solution.py:182
  521.0 38.5 %reduce.21 = bf16[4032,768]{1,0:T(8,128)(2,1)} reduce(bf16[4032,1,768]{2,1,0:T(2,128)(2,1)} %bitcast.274, bf16[]{:T(256)} %broadcast.533), dimensions={1}, to_apply=%bitcast.231.reduce_sub_computation | reduce | bytes 12386306
  559.5 8.3 reshape.509
  567.8 4.9 all-to-all-start.1
  573.3 135.2 %all-gather.2 = bf16[32,24,8]{1,2,0:T(8,128)(2,1)S(1)} all-gather(bf16[1,24,8]{1,2,0:T(8,128)(2,1)S(1)} %bitcast.296), channel_id=1, replica_groups=mesh['wide'=8,'tp'=4] {'wide','tp'}, dimensions={0}, use_global_device_ids=true | all-gather | bytes 12672 | tf_op jit(solution)/shard_map/all_gather | solution.py:110
  710.0 21.1 %gather_fusion.3 = bf16[4032,768]{1,0:T(8,128)(2,1)} fusion(bf16[1600,768]{1,0:T(8,128)(2,1)} %all-gather.12.cloned.1.call-done, s32[4096]{0:T(1024)S(1)} %pad_clamp_fusion.1), kind=kCustom, calls=%fused_computation.1.clone | custom fusion | bytes 12402432 | tf_op jit(solution)/shard_map/jit(_take)/gather | solution.py:196
  733.5 17.8 %gather_fusion.1 = f32[3200]{0:T(1024)S(1)} fusion(f32[1600,8]{0,1:T(8,128)S(1)} %fusion.102, s32[3200]{0:T(1024)S(1)} %reshape.415), kind=kCustom, calls=%fused_computation.3 | custom fusion | bytes 51200 | tf_op jit(solution)/shard_map/jit(take_along_axis)/gather | solution.py:161
  753.2 15.8 scatter_custom_fusion.1
  769.1 10.5 reshape.510
  779.6 9.5 fusion.19
  789.2 165.1 %all_to_all.16 = bf16[8,504,768]{2,1,0:T(8,128)(2,1)S(1)} all-to-all(bf16[8,504,768]{2,1,0:T(8,128)(2,1)S(1)} %bitcast.280), channel_id=1, replica_groups=mesh['wide'=8,'tp'=4] {'wide'}, dimensions={0} | all-to-all | bytes 12386304 | tf_op jit(solution)/shard_map/all_to_all | solution.py:202
  954.2 18.3 %convert_reduce_fusion.1 = (bf16[768]{0:T(1024)(128)(2,1)}, bf16[4032,768]{1,0:T(8,128)(2,1)}) fusion(f32[4032,768]{1,0:T(8,128)} %get-tuple-element.200, bf16[4032,768]{1,0:T(8,128)(2,1)S(1)} %bitcast.277, bf16[1,768,768]{2,1,0:T(8,128)(2,1)S(1)} %copy-done.60, f32[4032,768]{1,0:T(8,128)} %get-tuple-element.216, f32[768]{0:T(1024)S(1)} %copy-done.54), kind=kOutput, calls=%fused_computation.60 | convolution fusion | flops 4808981504 | bytes 38343168 | tf_op jit(solution)/shard_map/ecd,edf->ecf/dot_general | solution.py:203
  972.5 8.2 fusion.33
  980.7 45.7 %copy.213 = bf16[1,4032,768]{2,0,1:T(2,128)(2,1)} copy(bf16[1,4032,768]{2,1,0:T(8,128)(2,1)S(1)} %fusion.33) | data formatting | bytes 12386304 | tf_op jit(solution)/shard_map/convert_element_type | solution.py:212
  1026.4 38.6 %reduce.22 = bf16[4032,768]{1,0:T(8,128)(2,1)} reduce(bf16[4032,1,768]{2,1,0:T(2,128)(2,1)} %bitcast.275, bf16[]{:T(256)} %broadcast.533), dimensions={1}, to_apply=%bitcast.230.reduce_sub_computation | reduce | bytes 12386306
  1065.0 8.3 reshape.511
  1073.3 4.9 all-to-all-start.3
  1079.4 19.2 %gather_fusion = bf16[3200]{0:T(1024)(128)(2,1)S(1)} fusion(bf16[4032]{0:T(1024)(128)(2,1)S(1)} %get-tuple-element.209, s32[4096]{0:T(1024)S(1)} %pad_clamp_fusion), kind=kCustom, calls=%fused_computation.2 | custom fusion | bytes 25600 | tf_op jit(solution)/shard_map/jit(_take)/gather | solution.py:234
  1100.9 112.7 %all-to-all-done.3 = bf16[8,2,193536]{2,1,0:T(2,128)(2,1)} async-done(((bf16[8,2,193536]{2,1,0:T(2,128)(2,1)}), bf16[8,2,193536]{2,1,0:T(2,128)(2,1)}, u32[]{:S(2)}, u32[]{:S(2)}) %all-to-all-start.3) | async-done | bytes 6193184 | tf_op jit(solution)/shard_map/all_to_all | solution.py:211
  1213.7 10.5 reshape.512
  1224.2 33.7 %scatter_custom_fusion.3 = f32[1600,768]{1,0:T(8,128)} fusion(s32[4032]{0:T(1024)} %copy-done.25, bf16[1,4032,768]{2,0,1:T(2,128)(2,1)} %bitcast.276, f32[]{:T(128)} %constant.93.clone.1), kind=kCustom, calls=%fused_computation.57 | custom fusion | flops 6193152 | bytes 17302016 | tf_op jit(solution)/shard_map/scatter-add | solution.py:217
  1257.8 4.1 convert_element_type.223
  1261.9 39.5 %scatter_custom_fusion.2 = f32[1600,768]{1,0:T(8,128)} fusion(s32[4032]{0:T(1024)} %copy-done.25, f32[4032]{0:T(1024)S(1)} %scatter_custom_fusion.1, f32[]{:T(128)} %constant.93.clone.1, bf16[1,4032,768]{2,0,1:T(2,128)(2,1)} %bitcast.272), kind=kCustom, calls=%fused_computation.54 | custom fusion | flops 9289728 | bytes 17318144 | tf_op jit(solution)/shard_map/scatter-add | solution.py:190
  1301.5 4.1 convert_element_type.212
  1307.6 3.4 multiply_reduce_fusion.1
  1311.0 26.5 %reduce-scatter.19.cloned.1.call-done = bf16[400,768]{1,0:T(8,128)(2,1)} async-done(((bf16[1600,768]{1,0:T(8,128)(2,1)}), bf16[400,768]{1,0:T(8,128)(2,1)}) %reduce-scatter.19.cloned.1.call-update) | async-done | bytes 614416 | tf_op jit(solution)/shard_map/reduce_scatter | solution.py:134
  1337.5 3.5 fusion.96
  1343.1 24.7 %all-gather.14.cloned.1.call-done = bf16[1600,768]{1,0:T(8,128)(2,1)} async-done(((bf16[400,768]{1,0:T(8,128)(2,1)}), bf16[1600,768]{1,0:T(8,128)(2,1)}) %all-gather.14.cloned.1.call-update) | async-done | bytes 2457616 | tf_op jit(solution)/shard_map/all_gather | solution.py:131
  1371.3 3.7 convolution_convert_fusion.3
  1374.9 4.4 reshape.383
  1379.3 23.3 %while.23 = (s32[]{:T(128)}, bf16[2,3,4,200,3,64]{3,5,4,2,1,0:T(8,128)(2,1)}, bf16[2,3,4,200,3,64]{3,5,4,2,1,0:T(8,128)(2,1)S(1)}, f32[2,4,3,200,1]{3,2,1,4,0:T(...) while((s32[]{:T(128)}, ...), condition=%wide.region_28.30_spmd, body=%wide.region_26.29_spmd.sunk | while | flops 314896992 | bytes 30658964 | solution.py:264
  1381.2 3.0 fusion.147
  1384.9 2.8 multiply_reduce_fusion.7
  1392.8 3.0 fusion.147
  1396.5 2.8 multiply_reduce_fusion.7
  1402.6 3.5 copy.172
  1406.1 3.3 convert_element_type.232
  1409.4 5.0 fusion.50
  1419.5 5.3 bitcast_convert_fusion
  1426.3 3.7 convert_reduce_fusion
  1430.1 37.2 %all-reduce.6 = (bf16[768,8]{0,1:T(8,128)(2,1)S(1)}, bf16[192,8]{0,1:T(8,128)(2,1)S(1)}) all-reduce(bf16[768,8]{0,1:T(8,128)(2,1)S(1)} %bitcast.289, bf16[192,8]{0,1:T(8,128)(2,1)S(1)} %bitcast.292), channel_id=12, replica_groups=mesh['wide'=8,'tp'=4] {'wide'}, use_global_device_ids=true, to_apply=%region_44.46.clone | all-reduce | flops 7680 | bytes 30720
  1469.7 10.1 convolution_bitcast_fusion.1
  1479.8 10.0 convolution_bitcast_fusion.2
  1494.1 4.8 reduce-scatter.27.cloned.1.call-done
  1501.1 33.1 %reduce-scatter.23.cloned.1.call-done = bf16[400,768]{1,0:T(8,128)(2,1)} async-done(((bf16[1600,768]{1,0:T(8,128)(2,1)}), bf16[400,768]{1,0:T(8,128)(2,1)}) %reduce-scatter.23.cloned.1.call-update) | async-done | bytes 614416 | tf_op jit(solution)/shard_map/reduce_scatter | solution.py:134
  1536.0 40.3 %all-reduce.5 = (f32[2,768]{1,0:T(2,128)S(1)}, f32[5,768]{1,0:T(8,128)S(1)}, f32[8,768]{1,0:T(8,128)S(1)}) all-reduce(f32[2,768]{1,0:T(2,128)S(1)} %pad_maximum_fusion.1, f32[5,768]{1,0:T(8,128)S(1)} %pad_maximum_fusion, f32[8,768]{1,0:T(8,128)S(1)} %fusion.103), channel_id=7, replica_groups=mesh['wide'=8,'tp'=4] {'wide','tp'}, use_global_device_ids=true, to_apply=%region_34.36.clone | all-reduce | flops 11520 | bytes 92160
  (313 shorter events, 91.8 us)
Async XLA Ops:
  7.2 429.1 %copy-start = (bf16[1,768,768]{2,1,0:T(8,128)(2,1)S(1)}, bf16[1,768,768]{2,1,0:T(8,128)(2,1)}, u32[]{:S(2)}) copy-start(bf16[1,768,768]{2,1,0:T(8,128)(2,1)} %param.24) | copy-start | bytes 3538948
  7.2 87.8 %copy-start.22 = (bf16[3,96,192]{2,1,0:T(8,128)(2,1)S(1)}, bf16[3,96,192]{2,1,0:T(8,128)(2,1)}, u32[]{:S(2)}) copy-start(bf16[3,96,192]{2,1,0:T(8,128)(2,1)} %param.21) | copy-start | bytes 331780
  7.2 160.4 %all-gather.8.cloned.1.call-start = ((), (), s32[]{:S(2)}) async-start(), calls=%async_computation.11 | async-start | bytes 3072000 | tf_op jit(solution)/shard_map/all_gather | solution.py:131
  52.6 42.4 %copy-start.30 = (f32[400]{0:T(512)}, f32[400]{0:T(512)S(1)}, u32[]{:S(2)}) copy-start(f32[400]{0:T(512)S(1)} %broadcast_multiply_fusion.7) | copy-start | bytes 4804
  54.0 41.0 %copy-start.41 = (f32[400]{0:T(512)}, f32[400]{0:T(512)S(1)}, u32[]{:S(2)}) copy-start(f32[400]{0:T(512)S(1)} %add_rsqrt_fusion.1) | copy-start | bytes 4804
  94.9 39.4 %copy-start.33 = (bf16[192,96]{1,0:T(8,128)(2,1)S(1)}, bf16[192,96]{1,0:T(8,128)(2,1)}, u32[]{:S(2)}) copy-start(bf16[192,96]{1,0:T(8,128)(2,1)} %param.22) | copy-start | bytes 110596
  94.9 141.5 %reduce-scatter.17.cloned.1.call-start = ((), (), s32[]{:S(2)}) async-start(), calls=%async_computation.12 | async-start | bytes 3072000 | tf_op jit(solution)/shard_map/reduce_scatter | solution.py:134
  179.0 2.9 copy-start.32
  187.8 2.9 copy-start.32
  196.1 7.0 copy-start.3
  199.6 36.8 %copy-start.23 = (f32[768]{0:T(1024)S(1)}, f32[768]{0:T(1024)}, u32[]{:S(2)}) copy-start(f32[768]{0:T(1024)} %get-tuple-element.171) | copy-start | bytes 9220
  203.2 33.3 %copy-start.6 = (bf16[400,768]{1,0:T(8,128)(2,1)S(1)}, bf16[400,768]{1,0:T(8,128)(2,1)}, u32[]{:S(2)}) copy-start(bf16[400,768]{1,0:T(8,128)(2,1)} %param.18) | copy-start | bytes 1843204
  203.2 36.2 %copy-start.37 = (f32[768]{0:T(1024)S(1)}, f32[768]{0:T(1024)}, u32[]{:S(2)}) copy-start(f32[768]{0:T(1024)} %get-tuple-element.173) | copy-start | bytes 9220
  203.2 36.2 %copy-start.50 = (f32[768]{0:T(1024)S(1)}, f32[768]{0:T(1024)}, u32[]{:S(2)}) copy-start(f32[768]{0:T(1024)} %get-tuple-element.170) | copy-start | bytes 9220
  203.2 62.2 %all-gather.10.cloned.1.call-start = ((), (), s32[]{:S(2)}) async-start(), calls=%async_computation.13 | async-start | bytes 3072000 | tf_op jit(solution)/shard_map/all_gather | solution.py:131
  236.5 2.9 copy-start.12
  236.5 4.2 copy-start.18
  237.9 2.7 copy-start.43
  262.7 23.7 %copy-start.25 = (s32[4032]{0:T(1024)}, s32[4032]{0:T(1024)S(1)}, u32[]{:S(2)}) copy-start(s32[4032]{0:T(1024)S(1)} %compare_select_fusion.3) | copy-start | bytes 48388
  262.8 23.7 %copy-start.39 = (pred[4032]{0:T(1024)(128)(4,1)}, pred[4032]{0:T(1024)(128)(4,1)S(1)}, u32[]{:S(2)}) copy-start(pred[4032]{0:T(1024)(128)(4,1)S(1)} %compare_and_fusion) | copy-start | bytes 12100
  293.8 6.0 copy-start.58
  293.8 6.2 copy-start.55
  293.8 142.4 %all-to-all-start = ((bf16[8,504,768]{2,1,0:T(8,128)(2,1)}), bf16[8,504,768]{2,1,0:T(8,128)(2,1)}, u32[]{:S(2)}, u32[]{:S(2)}) async-start(bf16[8,504,768]{2,1,0:T(8,128)(2,1)} %bitcast.279), calls=%async_computation.1 | async-start | bytes 12386304 | tf_op jit(solution)/shard_map/all_to_all | solution.py:166
  300.1 169.4 %copy-start.53 = (f32[768]{0:T(1024)}, f32[768]{0:T(1024)S(1)}, u32[]{:S(2)}) copy-start(f32[768]{0:T(1024)S(1)} %convert_reduce_fusion.5) | copy-start | bytes 9220
  436.2 33.2 %copy-start.59 = (bf16[1,768,768]{2,1,0:T(8,128)(2,1)S(1)}, bf16[1,768,768]{2,1,0:T(8,128)(2,1)}, u32[]{:S(2)}) copy-start(bf16[1,768,768]{2,1,0:T(8,128)(2,1)} %param.26) | copy-start | bytes 3538948
  469.4 5.3 copy-start.62
  567.8 5.5 copy-start.56
  567.8 201.3 %all-to-all-start.1 = ((bf16[8,2,193536]{2,1,0:T(2,128)(2,1)}), bf16[8,2,193536]{2,1,0:T(2,128)(2,1)}, u32[]{:S(2)}, u32[]{:S(2)}) async-start(bf16[8,2,193536]{2,1,0:T(2,128)(2,1)} %reshape.509), calls=%async_computation.2 | async-start | bytes 12386304 | tf_op jit(solution)/shard_map/all_to_all | solution.py:181
  572.7 137.3 %all-gather.12.cloned.1.call-start = ((), (), s32[]{:S(2)}) async-start(), calls=%async_computation.15 | async-start | bytes 3072000 | tf_op jit(solution)/shard_map/all_gather | solution.py:131
  708.6 22.4 %copy-start.34 = (bf16[768,8]{0,1:T(8,128)(2,1)}, bf16[768,8]{0,1:T(8,128)(2,1)S(1)}, u32[]{:S(2)}) copy-start(bf16[768,8]{0,1:T(8,128)(2,1)S(1)} %reshape.467) | copy-start | bytes 36868
  733.5 18.9 %copy-start.19 = (s32[1600,2]{0,1:T(2,128)S(1)}, s32[1600,2]{0,1:T(2,128)}, u32[]{:S(2)}) copy-start(s32[1600,2]{0,1:T(2,128)} %param.28) | copy-start | bytes 38404
  733.5 19.0 %copy-start.36 = (f32[1600]{0:T(1024)S(1)}, f32[1600]{0:T(1024)}, u32[]{:S(2)}) copy-start(f32[1600]{0:T(1024)} %fusion.88) | copy-start | bytes 19204
  769.1 10.5 copy-start.40
  789.1 165.1 %copy-start.54 = (f32[768]{0:T(1024)S(1)}, f32[768]{0:T(1024)}, u32[]{:S(2)}) copy-start(f32[768]{0:T(1024)} %copy-done.53) | copy-start | bytes 9220
  789.1 165.1 %copy-start.60 = (bf16[1,768,768]{2,1,0:T(8,128)(2,1)S(1)}, bf16[1,768,768]{2,1,0:T(8,128)(2,1)}, u32[]{:S(2)}) copy-start(bf16[1,768,768]{2,1,0:T(8,128)(2,1)} %param.26) | copy-start | bytes 3538948
  954.2 18.3 %copy-start.9 = (bf16[8,504,768]{2,1,0:T(8,128)(2,1)}, bf16[8,504,768]{2,1,0:T(8,128)(2,1)S(1)}, u32[]{:S(2)}) copy-start(bf16[8,504,768]{2,1,0:T(8,128)(2,1)S(1)} %all_to_all.16) | copy-start | bytes 18579460
  1073.3 5.0 copy-start.21
  1073.3 140.4 %all-to-all-start.3 = ((bf16[8,2,193536]{2,1,0:T(2,128)(2,1)}), bf16[8,2,193536]{2,1,0:T(2,128)(2,1)}, u32[]{:S(2)}, u32[]{:S(2)}) async-start(bf16[8,2,193536]{2,1,0:T(2,128)(2,1)} %reshape.511), calls=%async_computation.5 | async-start | bytes 12386304 | tf_op jit(solution)/shard_map/all_to_all | solution.py:211
  1078.2 228.0 %reduce-scatter.25.cloned.1.call-start = ((), (), s32[]{:S(2)}) async-start(), calls=%async_computation.19 | async-start | bytes 512000
  1100.7 206.8 %reduce-scatter.21.cloned.1.call-start = ((), (), s32[]{:S(2)}) async-start(), calls=%async_computation.16 | async-start | bytes 3072000 | tf_op jit(solution)/shard_map/reduce_scatter | solution.py:236
  1261.9 75.6 %reduce-scatter.19.cloned.1.call-start = ((), (), s32[]{:S(2)}) async-start(), calls=%async_computation.14 | async-start | bytes 3072000 | tf_op jit(solution)/shard_map/reduce_scatter | solution.py:134
  1305.6 1.9 copy-start.24
  1305.6 2.0 copy-start.35
  1305.6 2.0 copy-start.38
  1305.6 2.0 copy-start.44
  1305.6 2.0 copy-start.48
  1305.6 31.9 %copy-start.16 = (bf16[400,768]{1,0:T(8,128)(2,1)S(1)}, bf16[400,768]{1,0:T(8,128)(2,1)}, u32[]{:S(2)}) copy-start(bf16[400,768]{1,0:T(8,128)(2,1)} %param.29) | copy-start | bytes 1843204
  1305.6 62.2 %all-gather.14.cloned.1.call-start = ((), (), s32[]{:S(2)}) async-start(), calls=%async_computation.17 | async-start | bytes 3072000 | tf_op jit(solution)/shard_map/all_gather | solution.py:131
  1307.4 33.6 %copy-start.45 = (bf16[400,8]{0,1:T(8,128)(2,1)}, bf16[400,8]{0,1:T(8,128)(2,1)S(1)}, u32[]{:S(2)}) copy-start(bf16[400,8]{0,1:T(8,128)(2,1)S(1)} %select_reduce_fusion) | copy-start | bytes 19204
  1341.1 26.8 %copy-start.15 = (bf16[1600,192]{0,1:T(8,128)(2,1)S(1)}, bf16[1600,192]{0,1:T(8,128)(2,1)}, u32[]{:S(2)}) copy-start(bf16[1600,192]{0,1:T(8,128)(2,1)} %reshape.374) | copy-start | bytes 1843204
  1343.0 149.5 %reduce-scatter.29.cloned.1.call-start = ((), (), s32[]{:S(2)}) async-start(), calls=%async_computation.21 | async-start | bytes 442368
  1371.2 8.1 copy-start.4
  1371.2 127.8 %reduce-scatter.27.cloned.1.call-start = ((), (), s32[]{:S(2)}) async-start(), calls=%async_computation.20 | async-start | bytes 1105920
  1384.9 2.8 copy-start.1
  1396.5 2.8 copy-start.1
  1419.2 115.0 %reduce-scatter.23.cloned.1.call-start = ((), (), s32[]{:S(2)}) async-start(), calls=%async_computation.18 | async-start | bytes 3072000 | tf_op jit(solution)/shard_map/reduce_scatter | solution.py:134
  1479.8 10.1 copy-start.49
  1479.8 10.1 copy-start.52
  1479.8 10.1 copy-start.51
  1489.8 44.4 %copy-start.8 = (bf16[400,768]{1,0:T(8,128)(2,1)S(1)}, bf16[400,768]{1,0:T(8,128)(2,1)}, u32[]{:S(2)}) copy-start(bf16[400,768]{1,0:T(8,128)(2,1)} %param.18) | copy-start | bytes 1843204
  1489.8 44.4 %copy-start.29 = (f32[768]{0:T(1024)S(1)}, f32[768]{0:T(1024)}, u32[]{:S(2)}) copy-start(f32[768]{0:T(1024)} %copy-done.28) | copy-start | bytes 9220
  1489.8 44.4 %copy-start.31 = (f32[400]{0:T(512)S(1)}, f32[400]{0:T(512)}, u32[]{:S(2)}) copy-start(f32[400]{0:T(512)} %copy-done.30) | copy-start | bytes 4804
  1489.8 44.4 %copy-start.42 = (f32[400]{0:T(512)S(1)}, f32[400]{0:T(512)}, u32[]{:S(2)}) copy-start(f32[400]{0:T(512)} %copy-done.41) | copy-start | bytes 4804
  1489.9 88.4 %copy-start.11 = (f32[400,768]{1,0:T(8,128)S(1)}, f32[400,768]{1,0:T(8,128)}, u32[]{:S(2)}) copy-start(f32[400,768]{1,0:T(8,128)} %copy-done.10) | copy-start | bytes 3686404
  (18 other events, 20.5 us)
Sparse Core Ops, SparseCore 0:
  95.0 22.0 all-gather.7
  203.3 33.0 reduce-scatter.16
  240.7 24.6 all-gather.9
  574.9 24.9 all-gather.11
  1100.8 21.2 reduce-scatter.24
  1262.0 31.7 reduce-scatter.20
  1305.7 31.7 reduce-scatter.18
  1343.2 24.6 all-gather.13
  1371.5 61.4 reduce-scatter.28
  1436.5 62.4 reduce-scatter.26
  1501.5 32.6 reduce-scatter.22
where the time goes:
time: 1600 us; the launch traced here: 1590 us
  blocking collectives  528 us (33%)
  waiting for transfers between devices  374 us (23%)
  local copies, waits for them, and re-layouts  302 us (19%)
  other arithmetic  213 us (13%)
  matrix products  137 us (9%)
  starting transfers between devices  17.2 us (1%)
    all_to_all x1, blocking collectives, body(): lax.all_to_all(slot_grads_all, 'wide', split_axis=0, concat_axis=1, tiled...  165 us
    all_to_all x1, waiting for transfers between devices, body(): lax.all_to_all(rows_all, 'wide', split_axis=0, concat_axis=1, tiled=True)  136 us
    all_gather x1, blocking collectives, body(): lax.all_gather(router_weight, ('wide', 'tp'), axis=1, tiled=True)  135 us
    all_to_all x1, waiting for transfers between devices, body(): lax.all_to_all(owned_grad_in.astype(jnp.bfloat16), 'wide', split_axis=1,...  113 us
    reduce_scatter x3, waiting for transfers between devices, from_group(): lax.psum_scatter(partial_rows.astype(jnp.bfloat16), 'tp', scatter_dimensi...  92.7 us
    unnamed x2, blocking collectives  77.5 us
    unnamed x3, other arithmetic  77.2 us
    unnamed x138, local copies, waits for them, and re-layouts  55.6 us
  transfers between devices with their start and end apart: 14, of which 8 were waited for; matrix products, arithmetic and copies ran while one was open for 18% of the time, Pallas kernels for 0%

commit v1 on v0

v1 whole, which is shorter than its diff:
```python
import functools

import jax
import jax.numpy as jnp
from jax import lax
from jax.experimental import pallas as pl
from jax.experimental.pallas import tpu as pltpu
from jax.sharding import PartitionSpec as P

D = 768
FF = 3072
HD = 64
SEQ = 200
VALID = 197
GROUP = 192
SLOTS = (608, 384)
WINDOW = 224
NARROW = 96
EPSILON = 1e-06
MASKED = -1000000000.0
F32 = jnp.float32
BF16 = jnp.bfloat16
VALID_LANE = 64
MIB = 1 << 20


def params(megabytes, sizes=None):
    semantics = None if sizes is None else ("arbitrary",) * sizes
    return pltpu.CompilerParams(
        vmem_limit_bytes=megabytes * MIB, dimension_semantics=semantics
    )


def cost(flops, moved, slow=0):
    return pl.CostEstimate(flops=int(flops), bytes_accessed=int(moved), transcendentals=int(slow))


def dot(left, right):
    return jnp.dot(left, right, preferred_element_type=F32)


def dot_nt(left, right):
    return lax.dot_general(left, right, (((1,), (1,)), ((), ())), preferred_element_type=F32)


def dot_tn(left, right):
    return lax.dot_general(left, right, (((0,), (0,)), ((), ())), preferred_element_type=F32)


def standardize(inputs):
    average = jnp.mean(inputs, axis=-1, keepdims=True)
    centered = inputs - average
    inverse = lax.rsqrt(jnp.mean(centered * centered, axis=-1, keepdims=True) + EPSILON)
    return centered * inverse, inverse


def norm_back(upstream, scaled, inverse, gain):
    grad_hat = upstream * gain
    mean_grad = jnp.mean(grad_hat, axis=-1, keepdims=True)
    mean_cross = jnp.mean(grad_hat * scaled, axis=-1, keepdims=True)
    return inverse * (grad_hat - mean_grad - scaled * mean_cross)


class Ring:
    def __init__(self, count):
        self.count = count
        self.half = count // 2
        self.order = list(range(0, count, 2)) + list(range(count - 1, 0, -2))
        self.ahead = [(self.order[i], self.order[(i + 1) % count]) for i in range(count)]
        self.behind = [(self.order[i], self.order[i - 1]) for i in range(count)]

    def sources(self):
        me = lax.axis_index("wide")
        place = jnp.where(me % 2 == 0, me // 2, self.count - 1 - me // 2)

        def at(position):
            position = position % self.count
            return jnp.where(
                position < self.half, 2 * position, 2 * (self.count - 1 - position) + 1
            )

        found = [at(place)]
        for step in range(1, self.half):
            found += [at(place - step), at(place + step)]
        return jnp.stack(found + [at(place + self.half)]).astype(jnp.int32)

    def forward(self, block):
        return lax.ppermute(block, "wide", self.ahead)

    def backward(self, block):
        return lax.ppermute(block, "wide", self.behind)

    def gather(self, block, cut):
        found = [block]
        left = right = block
        for _ in range(1, self.half):
            left, right = self.forward(left), self.backward(right)
            found += [left, right]
        return found, (self.forward(left[:cut]), self.backward(right[cut:]))

    def scatter_first(self, last, cut):
        return self.backward(last[:cut]), self.forward(last[cut:])

    def scatter_next(self, pair):
        return self.backward(pair[0]), self.forward(pair[1])


def to_core(block):
    return lax.ppermute(block, "tp", [(i, i ^ 1) for i in range(4)])


def to_x(block):
    return lax.ppermute(block, "tp", [(i, i ^ 2) for i in range(4)])


def assemble_kernel(count, rows, cut, source_ref, *refs):
    blocks, first, second, weights, small = (
        refs[: count - 1],
        refs[count - 1],
        refs[count],
        refs[count + 1],
        refs[count + 2],
    )
    for i in range(count - 1):
        weights[source_ref[i]] = blocks[i][0:rows]
        small[source_ref[i]] = blocks[i][rows:]
    last = source_ref[count - 1]
    weights[last, 0:cut] = first[...]
    if rows > cut:
        weights[last, cut:rows] = second[0 : rows - cut]
    small[last] = second[rows - cut :]


def attend_kernel(index, tokens, norms, bias, *refs):
    weights = refs[:4]
    normed_ref, qkv_ref, mixed_ref, sums_ref, residual_ref, second_ref = refs[-6:]
    inputs = tokens[index].astype(F32)
    scaled, _ = standardize(inputs)
    normed = (scaled * norms[0:1] + norms[2:3]).astype(BF16)
    normed_ref[...] = normed
    residual = inputs + norms[5:6]
    lane = lax.broadcasted_iota(jnp.int32, (SEQ, 128), 1)
    key_valid = lax.broadcasted_iota(jnp.int32, (SEQ, SEQ), 1) < VALID
    sums = jnp.zeros((SEQ, 128), F32)
    for j in range(4):
        projected = (dot(normed, weights[j][...]) + bias[j : j + 1]).astype(BF16)
        qkv_ref[j] = projected
        mixed = [jnp.zeros((SEQ, HD), BF16)]
        for h in range(3):
            query = projected[:, HD * h : HD * (h + 1)]
            key_rows = projected[:, GROUP + HD * h : GROUP + HD * (h + 1)]
            value = projected[:, 2 * GROUP + HD * h : 2 * GROUP + HD * (h + 1)]
            scores = jnp.where(key_valid, dot_nt(query, key_rows) * HD ** (-0.5), MASKED)
            row_max = jnp.max(scores, axis=-1, keepdims=True)
            exponent = jnp.exp(scores - row_max)
            row_sum = jnp.sum(exponent, axis=-1, keepdims=True)
            attention = (exponent / row_sum).astype(BF16)
            mixed.append(dot(attention, value).astype(BF16))
            sums = jnp.where(lane == 3 * j + h, row_max + jnp.log(row_sum), sums)
        mixed = jnp.concatenate(mixed, axis=1)
        mixed_ref[j] = mixed
        residual = residual + dot_nt(mixed, weights[j][:, D - 256 :])
    sums_ref[...] = sums
    residual_ref[...] = residual
    scaled_two, _ = standardize(residual)
    second = (scaled_two * norms[1:2] + norms[6:7]).astype(BF16)
    if index:
        second_ref[0] = refs[4][...]
        second_ref[1] = second
    else:
        second_ref[...] = second


def attend_back_kernel(
    index, tokens, cotangent, mine, left, right, residual, sums_ref, norms, *refs
):
    weights = refs[:4]
    qkv_ref, input_grad, branch_ref, grads_ref, small_ref, bias_ref = refs[4:]
    grad_two = mine[index].astype(F32) + left[index].astype(F32) + right[index].astype(F32)
    scaled_two, inverse_two = standardize(residual[...])
    grad_mid = cotangent[index].astype(F32) + norm_back(
        grad_two, scaled_two, inverse_two, norms[1:2]
    )
    branch = grad_mid.astype(BF16)
    branch_ref[...] = branch
    key_valid = lax.broadcasted_iota(jnp.int32, (SEQ, SEQ), 1) < VALID
    grad_one = jnp.zeros((SEQ, D), F32)
    scale = HD ** (-0.5)
    for j in range(4):
        upstream = dot(branch, weights[j][:, D - 256 :]).astype(BF16)
        grads = [[], [], []]
        for h in range(3):
            query = qkv_ref[j, :, HD * h : HD * (h + 1)]
            key_rows = qkv_ref[j, :, GROUP + HD * h : GROUP + HD * (h + 1)]
            value = qkv_ref[j, :, 2 * GROUP + HD * h : 2 * GROUP + HD * (h + 1)]
            up = upstream[:, HD * (h + 1) : HD * (h + 2)]
            scores = jnp.where(key_valid, dot_nt(query, key_rows) * scale, MASKED)
            attention = jnp.exp(scores - sums_ref[:, 3 * j + h : 3 * j + h + 1])
            grad_attn = dot_nt(up, value)
            inner = jnp.sum(attention * grad_attn, axis=-1, keepdims=True)
            grad_scores = (attention * (grad_attn - inner)).astype(BF16)
            grads[0].append((dot(grad_scores, key_rows) * scale).astype(BF16))
            grads[1].append((dot_tn(grad_scores, query) * scale).astype(BF16))
            grads[2].append(dot_tn(attention.astype(BF16), up).astype(BF16))
        whole = jnp.concatenate(
            grads[0] + grads[1] + grads[2] + [jnp.zeros((SEQ, GROUP), BF16)], axis=1
        )
        grads_ref[j] = whole
        bias_ref[j : j + 1] = jnp.sum(whole.astype(F32), axis=0, keepdims=True)
        grad_one = grad_one + dot_nt(whole, weights[j][...])
    scaled_one, inverse_one = standardize(tokens[index].astype(F32))
    input_grad[...] = grad_mid + norm_back(grad_one, scaled_one, inverse_one, norms[0:1])
    small_ref[...] = jnp.concatenate(
        [
            jnp.sum(part, axis=0, keepdims=True)
            for part in (
                grad_one * scaled_one,
                grad_two * scaled_two,
                grad_one,
                grad_mid,
                grad_two,
            )
        ]
        + [jnp.zeros((3, D), F32)],
        axis=0,
    )


def weight_grad_kernel(groups, places, rows, sources, *refs):
    normed, grads, branch, mixed = refs[0:2], refs[2:4], refs[4:6], refs[6:8]
    outs, whole = refs[8:-1], refs[-1]
    for out, j in zip(outs, groups):
        whole[...] = dot_tn(normed[0][...], grads[0][j]) + dot_tn(normed[1][...], grads[1][j])
        whole[:, D - 256 :] += dot_tn(branch[0][...], mixed[0][j]) + dot_tn(
            branch[1][...], mixed[1][j]
        )
        for i, place in enumerate(places):
            start = pl.multiple_of(sources[place] * rows, 8)
            block = whole[pl.ds(start, rows)]
            missing = out.shape[1] - rows
            if missing:
                block = jnp.concatenate([block, jnp.zeros((missing, D), F32)], axis=0)
            out[i] = block.astype(BF16)


def pick_kernel(plan, slots, size_ref, offset_ref, places_ref, *refs):
    outs = refs[-len(plan) :]

    def clear(tile, carry):
        start = pl.multiple_of(tile * slots, 16)
        for out in outs:
            out[pl.ds(start, slots)] = jnp.zeros((slots, out.shape[1]), BF16)
        return carry

    lax.fori_loop(0, tiles_of(size_ref[0], slots), clear, 0)

    def some(i, base, height):
        slot = lax.broadcasted_iota(jnp.int32, (height, SEQ), 0) + base
        chosen = (places_ref[i : i + 1] == slot).astype(F32).astype(BF16)
        for out, stream in zip(outs, plan):
            which, index = stream[i]
            window = out.at[pl.ds(base, height)]
            window[...] += dot(chosen, refs[which][index]).astype(BF16)

    count = len(plan[0])
    for i in range(count):
        base = pl.multiple_of(offset_ref[i] // 16 * 16, 16)
        some(i, base, NARROW)
        pl.when(offset_ref[i + 1] > base + NARROW)(
            functools.partial(some, i, pl.multiple_of(base + NARROW, 16), WINDOW - NARROW)
        )


def unpick_kernel(size_ref, offset_ref, places_ref, slots_ref, *outs):
    def some(i, base, height):
        slot = lax.broadcasted_iota(jnp.int32, (height, SEQ), 0) + base
        chosen = (places_ref[i : i + 1] == slot).astype(F32).astype(BF16)
        row = lax.broadcasted_iota(jnp.int32, (height, D), 0) + base
        window = slots_ref[pl.ds(base, height)]
        window = jnp.where(row < size_ref[0], window, jnp.zeros_like(window))
        return dot_tn(chosen, window).astype(BF16)

    for i in range(2 * len(outs)):
        out = outs[i // 2].at[i % 2]
        base = pl.multiple_of(offset_ref[i] // 16 * 16, 16)
        out[...] = some(i, base, NARROW)

        @pl.when(offset_ref[i + 1] > base + NARROW)
        def _(i=i, out=out, base=base):
            more = pl.multiple_of(base + NARROW, 16)
            out[...] += some(i, more, WINDOW - NARROW)


def tiles_of(size, slots):
    return jnp.maximum(1, (size + slots - 1) // slots)


def moved(semaphores, *pairs):
    copies = [
        pltpu.make_async_copy(source, target, semaphores.at[i])
        for i, (source, target) in enumerate(pairs)
    ]
    for copy in copies:
        copy.start()
    for copy in copies:
        copy.wait()


def weight_block(which):
    return pl.BlockSpec((None, D, D), lambda f: (f, which, 0))


def expert_kernel(
    size, rows_hbm, grads_hbm, chosen_hbm, weights_hbm, second_bias, router,
    hidden_hbm, pre_hbm, gates_hbm, back_hbm, router_ref, bias_ref,
    rows, grads, chosen, gates, total, semaphores,
):
    slots = rows.shape[0]
    router_ref[...] = jnp.zeros_like(router_ref)
    bias_ref[...] = jnp.zeros_like(bias_ref)

    def tile(m, carry):
        at = pl.ds(pl.multiple_of(m * slots, 16), slots)
        moved(
            semaphores,
            (rows_hbm.at[at], rows),
            (grads_hbm.at[at], grads),
            (chosen_hbm.at[at], chosen),
        )
        lane = lax.broadcasted_iota(jnp.int32, (slots, 128), 1)
        signs = jnp.where(lane < VALID_LANE, chosen[...].astype(F32), 0.0)
        is_valid = chosen[:, VALID_LANE : VALID_LANE + 1].astype(F32)
        gap = jnp.sum(dot_nt(rows[...], router[...]) * signs, axis=1, keepdims=True)
        weight = is_valid / (1.0 + jnp.exp(-gap))
        slope = weight / (1.0 + jnp.exp(gap))
        direct = jnp.sum(grads[...].astype(F32) * second_bias[0:1], axis=1, keepdims=True)
        gates[...] = jnp.where(lane == 0, weight, jnp.where(lane == 1, slope, direct))
        total[...] = jnp.zeros_like(total)

        def step(first, second, first_bias, hidden_ref, pre_ref):
            pre = dot(rows[...], first[...]) + first_bias[0:1].astype(F32)
            back = dot(grads[...], second[...])
            below = 0.5 * (1.0 + lax.erf(pre * 0.5**0.5))
            density = jnp.exp(-0.5 * pre * pre) * (0.5 / 3.141592653589793) ** 0.5
            hidden = pre * below
            weight = gates[:, 0:1]
            added = jnp.sum(hidden * back, axis=1, keepdims=True)
            slope_pre = (weight * back * (below + pre * density)).astype(BF16)
            hidden_ref[...] = (weight * hidden).astype(BF16)
            pre_ref[...] = slope_pre
            gates[...] += jnp.where(lane == 2, added, 0.0)
            total[...] += dot_nt(slope_pre, first[...])

        part = pl.BlockSpec((slots, D), lambda f: (m, f))
        pltpu.emit_pipeline(
            step,
            grid=(FF // D,),
            in_specs=[
                weight_block(0),
                weight_block(1),
                pl.BlockSpec((None, 16, D), lambda f: (f, 2 * D // 16, 0)),
            ],
            out_specs=[part, part],
        )(weights_hbm, weights_hbm, weights_hbm, hidden_hbm, pre_hbm)
        logits_grad = (signs * gates[:, 1:2] * gates[:, 2:3]).astype(BF16)
        router_ref[...] += dot_tn(logits_grad, rows[...])
        bias_ref[0:1] += jnp.sum(weight * grads[...].astype(F32), axis=0, keepdims=True)
        rows[...] = (total[...] + dot(logits_grad, router[...])).astype(BF16)
        moved(semaphores, (rows, back_hbm.at[at]), (gates, gates_hbm.at[at]))
        return carry

    lax.fori_loop(0, tiles_of(size[0], slots), tile, 0)


def expert_rest_kernel(earlier, size, *refs):
    rows_hbm, grads_hbm, hidden_hbm, pre_hbm, gates_hbm, weights_hbm, second_bias = refs[:7]
    grad_hbm, result_hbm, rows, grads, gates, total, semaphores = refs[7 + earlier :]
    slots = rows.shape[0]

    def tile(m, carry):
        at = pl.ds(pl.multiple_of(m * slots, 16), slots)
        moved(
            semaphores,
            (rows_hbm.at[at], rows),
            (grads_hbm.at[at], grads),
            (gates_hbm.at[at], gates),
        )
        total[...] = gates[:, 0:1] * second_bias[0:1]

        def step(second, hidden, pre, *rest):
            out = rest[-1]
            total[...] += dot_nt(hidden[...], second[...])
            one = dot_tn(rows[...], pre[...])
            two = dot_tn(grads[...], hidden[...])
            sums = jnp.sum(pre[...].astype(F32), axis=0, keepdims=True)
            if len(rest) > 1:
                one = one + rest[0][0:D].astype(F32)
                two = two + rest[0][D : 2 * D].astype(F32)
                sums = sums + rest[0][2 * D : 2 * D + 1].astype(F32)
            out[0:D] = one.astype(BF16)
            out[D : 2 * D] = two.astype(BF16)
            out[2 * D :] = jnp.broadcast_to(sums, (16, D)).astype(BF16)

        def run(adds):
            part = pl.BlockSpec((slots, D), lambda f: (m, f))
            whole = pl.BlockSpec((None, 2 * D + 16, D), lambda f: (f, 0, 0))
            pltpu.emit_pipeline(
                step,
                grid=(FF // D,),
                in_specs=[weight_block(1), part, part] + [whole] * adds,
                out_specs=[whole],
            )(weights_hbm, hidden_hbm, pre_hbm, *[grad_hbm] * adds, grad_hbm)

        if earlier:
            run(True)
        else:
            pl.when(m == 0)(functools.partial(run, False))
            pl.when(m > 0)(functools.partial(run, True))
        rows[...] = total[...].astype(BF16)
        moved(semaphores, (rows, result_hbm.at[at]))
        return carry

    lax.fori_loop(0, tiles_of(size[0], slots), tile, 0)


def pack_kernel(first, second, small, out):
    out[0:D] = first[0]
    out[D : 2 * D] = second[0]
    out[2 * D :] = small[...]


def ring_add_kernel(is_first, mine_left, left, mine_right, right, out_left, out_right):
    def sums(one, other):
        return (one.astype(F32) + other.astype(F32)).astype(BF16)

    if is_first:
        out_left[0] = sums(mine_left[0], left[0])
        out_left[1] = mine_left[1]
        out_right[0] = mine_right[0]
        out_right[1] = sums(mine_right[1], right[0])
    else:
        out_left[...] = sums(mine_left[...], left[...])
        out_right[...] = sums(mine_right[...], right[...])


def sum_parts_kernel(one, other, *outs):
    start = 0
    for out in outs:
        part = slice(start, start + out.shape[0])
        out[...] = (one[part].astype(F32) + other[part].astype(F32)).astype(BF16)
        start += out.shape[0]


def tail_kernel(cut, entries, sources, small, *refs):
    outs = refs[-len(entries) :]
    refs = list(refs[: -len(entries)])
    near, far = refs.pop(0), refs.pop(0)
    rows = near.shape[1]
    for (place, index, kind), out in zip(entries, outs):
        whole = jnp.concatenate(
            [
                near[index].astype(F32) + far[index].astype(F32),
                small[sources[place]].astype(F32),
            ],
            axis=0,
        )
        if kind == "none":
            out[...] = whole.astype(out.dtype)
        elif kind == "low":
            out[0:cut] = (whole[0:cut] + refs.pop(0)[...].astype(F32)).astype(BF16)
            out[cut:] = whole[cut:].astype(BF16)
        elif kind == "high":
            out[0:cut] = whole[0:cut].astype(BF16)
            out[cut:] = (whole[cut:] + refs.pop(0)[...].astype(F32)).astype(BF16)
        elif kind == "full":
            out[...] = (whole + refs.pop(0)[...].astype(F32)).astype(BF16)
        else:
            left, right = refs.pop(0), refs.pop(0)
            out[...] = whole + left[...].astype(F32) + right[...].astype(F32)


def nothing_kernel(*refs):
    pass


SMEM = pl.BlockSpec(memory_space=pltpu.SMEM)
VMEM = pl.BlockSpec(memory_space=pltpu.VMEM)
ANY = pl.BlockSpec(memory_space=pl.ANY)


def shape(dims, kind=BF16):
    return jax.ShapeDtypeStruct(dims, kind)


def call(kernel, operands, specs, out_shape, out_specs, earlier=(), **settings):
    size = len(operands)
    waits = len(earlier)

    def stripped(*refs):
        kernel(*refs[:size], *refs[size + waits :])

    megabytes = settings.pop("megabytes", 32)
    work = settings.pop("work", (1e6, 1e6))
    return pl.pallas_call(
        stripped,
        in_specs=list(specs) + [ANY] * waits,
        out_specs=out_specs,
        out_shape=out_shape,
        compiler_params=params(megabytes),
        cost_estimate=cost(*work),
        **settings,
    )(*operands, *earlier)


def assemble(blocks, parts, sources, rows, cut):
    count = len(blocks) + 1
    tall = blocks[0].shape[0]
    return call(
        functools.partial(assemble_kernel, count, rows, cut),
        [sources, *blocks, *parts],
        [SMEM] + [VMEM] * (count + 1),
        [shape((count, rows, D)), shape((count, tall - rows, D))],
        [VMEM, VMEM],
        megabytes=16,
    )


def attend(tokens, index, norms, bias, weights, earlier, other=None):
    more = [] if other is None else [other]
    return call(
        functools.partial(attend_kernel, index),
        [tokens, norms, bias, *weights, *more],
        [VMEM] * (7 + len(more)),
        [
            shape((SEQ, D)),
            shape((4, SEQ, D)),
            shape((4, SEQ, 256)),
            shape((SEQ, 128), F32),
            shape((SEQ, D), F32),
            shape((2, SEQ, D) if more else (SEQ, D)),
        ],
        [VMEM] * 6,
        earlier,
        work=(6e9, 9e6),
    )


def attend_back(
    tokens, cotangent, index, parts, residual, sums, norms, weights, qkv, earlier
):
    return call(
        functools.partial(attend_back_kernel, index),
        [tokens, cotangent, *parts, residual, sums, norms, *weights, qkv],
        [VMEM] * 13,
        [
            shape((SEQ, D), F32),
            shape((SEQ, D)),
            shape((4, SEQ, D)),
            shape((8, D), F32),
            shape((4, D), F32),
        ],
        [VMEM] * 5,
        earlier,
        work=(8e9, 9e6),
    )


def weight_grads(normed, grads, branch, mixed, groups, places, sources, rows, rows_up, earlier):
    return call(
        functools.partial(weight_grad_kernel, groups, places, rows),
        [sources, *normed, *grads, *branch, *mixed],
        [SMEM] + [VMEM] * 8,
        [shape((len(places), rows_up, D))] * len(groups),
        [VMEM] * len(groups),
        earlier,
        scratch_shapes=[pltpu.VMEM((D, D), F32)],
        work=(2e9, 5e6),
    )


def sum_parts(one, other, sizes):
    return call(
        sum_parts_kernel,
        [one, other],
        [VMEM] * 2,
        [shape((size,) + one.shape[1:]) for size in sizes],
        [VMEM] * len(sizes),
    )


def tail(entries, sources, small, near, far, received, cut, kind=BF16):
    tall = near.shape[1] + small.shape[1]
    return call(
        functools.partial(tail_kernel, cut, entries),
        [sources, small, near, far, *received],
        [SMEM] + [VMEM] * (3 + len(received)),
        [shape((tall, D), kind)] * len(entries),
        [VMEM] * len(entries),
    )


def pick(size, offsets, places, sources, plan, widths, slots, most, earlier=()):
    return call(
        functools.partial(pick_kernel, plan, slots),
        [size, offsets, places, *sources],
        [SMEM, SMEM, VMEM] + [VMEM] * len(sources),
        [shape((most, width)) for width in widths],
        [VMEM] * len(widths),
        earlier,
        megabytes=48,
        work=(3e9, 6e6),
    )


def unpick(size, offsets, places, slots, earlier=()):
    count = places.shape[0] // 2
    return call(
        unpick_kernel,
        [size, offsets, places, slots],
        [SMEM, SMEM, VMEM, VMEM],
        [shape((2, SEQ, D))] * count,
        [VMEM] * count,
        earlier,
        megabytes=48,
        work=(3e9, 6e6),
    )


def expert(size, rows, grads, chosen, weights, second_bias, router, slots, earlier=()):
    most = rows.shape[0]
    return call(
        expert_kernel,
        [size, rows, grads, chosen, weights, second_bias, router],
        [SMEM, ANY, ANY, ANY, ANY, VMEM, VMEM],
        [
            shape((most, FF)),
            shape((most, FF)),
            shape((most, 128), F32),
            shape((most, D)),
            shape((128, D), F32),
            shape((8, D), F32),
        ],
        [ANY] * 4 + [VMEM] * 2,
        earlier,
        scratch_shapes=[
            pltpu.VMEM((slots, D), BF16),
            pltpu.VMEM((slots, D), BF16),
            pltpu.VMEM((slots, 128), BF16),
            pltpu.VMEM((slots, 128), F32),
            pltpu.VMEM((slots, D), F32),
            pltpu.SemaphoreType.DMA((3,)),
        ],
        megabytes=48,
        work=(1.4e10, 2e7),
    )


def expert_rest(size, side, weights, second_bias, slots, grad=None, earlier=()):
    most = side[0].shape[0]
    more = [] if grad is None else [grad]
    return call(
        functools.partial(expert_rest_kernel, len(more)),
        [size, *side, weights, second_bias, *more],
        [SMEM] + [ANY] * 6 + [VMEM] + [ANY] * len(more),
        [shape((4, 2 * D + 16, D)), shape((most, D))],
        [ANY, ANY],
        earlier,
        input_output_aliases={8: 0} if more else {},
        scratch_shapes=[
            pltpu.VMEM((slots, D), BF16),
            pltpu.VMEM((slots, D), BF16),
            pltpu.VMEM((slots, 128), F32),
            pltpu.VMEM((slots, D), F32),
            pltpu.SemaphoreType.DMA((3,)),
        ],
        megabytes=48,
        work=(1.4e10, 3e7),
    )


def pack(first, second, small, earlier):
    return call(
        pack_kernel,
        [first, second, small],
        [VMEM] * 3,
        shape((2 * D + 16, D)),
        VMEM,
        earlier,
    )


def ring_add(blocks, received, is_first, earlier=()):
    return call(
        functools.partial(ring_add_kernel, is_first),
        [blocks[0], received[0], blocks[1], received[1]],
        [VMEM] * 4,
        [shape(blocks[0].shape)] * 2,
        [VMEM] * 2,
        earlier,
    )


def after(value, *earlier):
    return call(
        nothing_kernel,
        [value],
        [ANY],
        shape(value.shape, value.dtype),
        ANY,
        earlier,
        input_output_aliases={0: 0},
        work=(0, 0),
    )


def body(
    count,
    tokens,
    norm_gains,
    shifts,
    attn_weight,
    out_weight,
    router_weight,
    expert_in,
    expert_in_bias,
    expert_down,
    expert_down_bias,
    routes,
    cotangent,
):
    ring = Ring(count)
    sources = ring.sources()
    wide, tp = lax.axis_index("wide"), lax.axis_index("tp")
    core, far = tp % 2, tp // 2
    rows = D // count
    rows_up = -(-rows // 16) * 16
    experts = router_weight.shape[0]
    group_rows = routes.shape[0]
    local_rows = tokens.shape[0]
    capacity = (10 * group_rows // (4 * experts) + 7) // 8 * 8
    near_steps = max(1, 5 * ring.half // 8)
    near_groups = 1 + 2 * near_steps
    sides = ((0, near_groups), (near_groups, count))
    most = [
        -(-(stop - start) * min(local_rows, capacity) // slots) * slots + WINDOW
        for (start, stop), slots in zip(sides, SLOTS)
    ]
    smalls = 7 + experts
    columns = D // count

    small = jnp.concatenate([norm_gains, shifts, router_weight], axis=0)
    near = to_core(small)
    small = jnp.where(
        core == 0,
        jnp.concatenate([small, near], axis=1),
        jnp.concatenate([near, small], axis=1),
    )
    near = to_x(small)
    small = jnp.where(
        far == 0,
        jnp.concatenate([small, near], axis=1),
        jnp.concatenate([near, small], axis=1),
    )
    small = jnp.pad(small.reshape(-1), (0, 2 * D - smalls * columns)).reshape(2, D)
    own_routes = lax.dynamic_slice_in_dim(routes, tp * local_rows, local_rows, 0)
    own_routes = jnp.pad(own_routes.T.astype(BF16), ((0, 0), (0, D - local_rows)))
    square = jnp.concatenate(
        [attn_weight[0], attn_weight[1], attn_weight[2], out_weight.T], axis=1
    )
    block = jnp.concatenate(
        [
            jnp.pad(square, ((0, rows_up - rows), (0, 0))),
            small,
            own_routes,
            jnp.zeros((12, D), BF16),
        ],
        axis=0,
    )
    tall = block.shape[0]
    cut = (tall // 2 + 15) // 16 * 16
    blocks, ends = ring.gather(block, cut)
    own, gathered_small = assemble(blocks, ends, sources, rows_up, cut)
    own = own[:, :rows].reshape(D, D)
    beside, across = to_core(own), to_x(own)
    opposite = to_core(across)
    weights = (own, beside, across, opposite)

    norms = (
        gathered_small[:, 0:2]
        .reshape(count, 2 * D)[:, : smalls * columns]
        .reshape(count, smalls, columns)
        .transpose(1, 0, 2)
        .reshape(smalls, D)
        .astype(F32)
    )
    router = jnp.pad(norms[7:].astype(BF16), ((0, 128 - experts), (0, 0)))

    def relative(values):
        values = values.reshape(2, 2, GROUP)
        values = jnp.where(far == 0, values, values[::-1])
        return jnp.where(core == 0, values, values[:, ::-1]).reshape(4, GROUP)

    nothing = jnp.zeros((4, GROUP), F32)
    bias = jnp.concatenate([relative(norms[3]), nothing, relative(norms[4]), nothing], axis=1)

    expert_block = jnp.concatenate(
        [
            expert_in_bias,
            jnp.pad(expert_down_bias, ((0, 0), (0, D - GROUP))),
            jnp.zeros((14, D), BF16),
        ],
        axis=0,
    )
    expert_block = pack(expert_in, expert_down, expert_block, [across])
    expert_all = lax.all_gather(expert_block, "tp", axis=0, tiled=True).reshape(4, -1, D)
    second_bias = jnp.broadcast_to(
        expert_all[:, 2 * D + 1, :GROUP].reshape(1, D).astype(F32), (8, D)
    )

    named = jnp.stack(
        [b[rows_up + 2 : rows_up + 4, :local_rows] for b in blocks]
        + [ends[1][rows_up + 2 - cut : rows_up + 4 - cut, :local_rows]]
    ).astype(F32)
    named = named.reshape(count, 2, 2, SEQ).transpose(1, 0, 2, 3).reshape(2, 2 * count, SEQ)
    mine = wide.astype(F32)
    is_first, is_second = named[0] == mine, named[1] == mine
    is_chosen = (is_first | is_second).astype(F32)
    other = jnp.where(is_first, named[1], named[0])
    lower = (jnp.arange(SEQ)[:, None] < jnp.arange(SEQ)[None, :]).astype(F32)
    rank = jnp.dot(is_chosen, lower)
    counts = jnp.sum(is_chosen, axis=-1)
    lane = jnp.arange(128).astype(F32)
    signs = (lane == mine).astype(F32) - (lane == other[..., None]).astype(F32)
    is_valid = (jnp.arange(SEQ) < VALID).astype(F32)
    signs = jnp.where(lane == VALID_LANE, is_valid[None, :, None], signs).astype(BF16)
    tables = []
    for start, stop in sides:
        part = slice(2 * start, 2 * stop)
        size = 2 * (stop - start)
        lower = jnp.arange(size)[:, None] < jnp.arange(size + 1)[None, :]
        offsets = jnp.sum(counts[part, None] * lower, axis=0)
        places = jnp.where(is_chosen[part] > 0, offsets[:size, None] + rank[part], -1.0)
        tables.append((
            offsets[size:].astype(jnp.int32), offsets.astype(jnp.int32), places.astype(jnp.int32)
        ))

    tokens = tokens.reshape(2, SEQ, D)
    cotangent = after(cotangent.reshape(2, SEQ, D), *ends)
    grad_blocks, grad_ends = ring.gather(cotangent, 1)
    first = attend(tokens, 0, norms, bias, weights, grad_blocks[3:5])
    second = attend(tokens, 1, norms, bias, weights, grad_blocks[-2:], first[5])
    forward = (first, second)

    def picked(side, blocks, last, widths, extra, earlier):
        start, stop = sides[side]
        groups = range(start, min(stop, count - 1))
        sources_ = [blocks[g] for g in groups]
        images = [(3 + i, index) for i in range(len(groups)) for index in range(2)]
        if stop == count:
            images += [(3 + len(groups), 0), (4 + len(groups), 0)]
            sources_ += list(last)
        plan = [[(which - 3, index) for which, index in images]]
        if extra is not None:
            plan.append([(len(sources_), 2 * start + i) for i in range(len(images))])
            sources_.append(extra)
        return pick(
            *tables[side], sources_, plan, widths, SLOTS[side], most[side], earlier
        )

    row_blocks, row_ends = ring.gather(second[5], 1)
    grad_slots = [
        picked(side, grad_blocks, grad_ends, (D, 128), signs, [second[0]]) for side in range(2)
    ]
    near_rows, = picked(0, row_blocks, row_ends, (D,), None, [])
    near = expert(
        tables[0][0], near_rows, *grad_slots[0], expert_all, second_bias, router, SLOTS[0],
        [grad_slots[1][0]],
    )
    far_rows, = picked(1, row_blocks, row_ends, (D,), None, [near[3]])
    distant = expert(
        tables[1][0], far_rows, *grad_slots[1], expert_all, second_bias, router, SLOTS[1]
    )
    router_grad = (near[4] + distant[4])[:experts]
    bias_grad = near[5][0] + distant[5][0]
    far_back = unpick(*tables[1], distant[3])
    near_back = unpick(*tables[0], near[3], [far_back[0]])

    def send_back(blocks, start, waits):
        pair = ring.scatter_first(start, 1)
        for step in range(ring.half - 1, 0, -1):
            total = ring_add(
                blocks[2 * step - 1 : 2 * step + 1], pair, step == ring.half - 1
            )
            waits(ring.half - 1 - step, total)
            pair = ring.scatter_next(total)
        return blocks[0], pair[0], pair[1]

    kept = {}

    def meanwhile(step, total):
        if step == 0:
            kept["near"] = expert_rest(
                tables[0][0],
                (near_rows, grad_slots[0][0], *near[:3]),
                expert_all,
                second_bias,
                SLOTS[0],
                None,
                total,
            )
        if step == 1:
            kept["far"] = expert_rest(
                tables[1][0],
                (far_rows, grad_slots[1][0], *distant[:3]),
                expert_all,
                second_bias,
                SLOTS[1],
                kept["near"][0],
                total,
            )
        if step == ring.half - 2:
            far_result = unpick(*tables[1], kept["far"][1], total)
            kept["result"] = unpick(*tables[0], kept["near"][1], [far_result[0]]) + far_result

    returned = send_back(near_back + far_back, far_back[-1], meanwhile)
    results = kept["result"]
    expert_grad = kept["far"][0]
    expert_grad = expert_grad.at[:, 2 * D + 1, :GROUP].set(
        bias_grad.reshape(4, GROUP).astype(BF16)
    )
    expert_grad = lax.psum_scatter(
        expert_grad.reshape(-1, D), "tp", scatter_dimension=0, tiled=True
    ).astype(F32)

    backward = []

    def attention_back(index, earlier):
        backward.append(
            attend_back(
                tokens, cotangent, index, returned, forward[index][4], forward[index][3], norms,
                weights, forward[index][1], earlier,
            )
        )

    def meanwhile(step, total):
        if step < 2:
            attention_back(step, total)

    start = after(results[-1], returned[1], returned[2])
    result = send_back(results, start, meanwhile)
    outputs = sum(part.astype(F32) for part in result)
    outputs = [(forward[i][4] + outputs[i]).astype(BF16) for i in range(2)]

    normed = [f[0] for f in forward]
    mixed = [f[2] for f in forward]
    branch = [b[1] for b in backward]
    grads = [b[2] for b in backward]
    order = [count - 1]
    for step in range(ring.half - 1, 0, -1):
        order += [2 * step - 1, 2 * step]
    order.append(0)
    sizes = (3 * count // 8, count // 4, count - 3 * count // 8 - count // 4)
    settings = (order, sources, rows, rows_up)
    opposite, across = weight_grads(normed, grads, branch, mixed, (3, 2), *settings, [])
    beside, own = weight_grads(normed, grads, branch, mixed, (1, 0), *settings, [across])
    far_parts = [to_x(part) for part in sum_parts(across, to_core(opposite), sizes)]
    near_parts = sum_parts(own, to_core(beside), sizes)

    def absolute(values):
        values = values.reshape(2, 2, GROUP)
        values = jnp.where(core == 0, values, values[:, ::-1])
        return jnp.where(far == 0, values, values[::-1]).reshape(1, D)

    sums = backward[0][3] + backward[1][3]
    bias_sums = backward[0][4] + backward[1][4]
    small = jnp.concatenate(
        [
            sums[0:3],
            absolute(bias_sums[:, :GROUP]),
            absolute(bias_sums[:, 2 * GROUP : 3 * GROUP]),
            sums[3:5],
            router_grad,
        ],
        axis=0,
    )
    small = small + to_core(small)
    small = small + to_x(small)
    small = small.reshape(smalls, count, columns).transpose(1, 0, 2).reshape(count, -1)
    small = jnp.pad(small, ((0, 0), (0, 16 * D - smalls * columns)))
    small = small.reshape(count, 16, D).astype(BF16)
    cut = (tall // 2 + 15) // 16 * 16
    found = [(part, i) for part in range(3) for i in range(sizes[part])]

    def step_of(entries, received, kind=BF16):
        part = found[entries[0][0]][0]
        return tail(
            [(order[at], found[at][1], how) for at, how in entries],
            sources,
            small,
            near_parts[part],
            far_parts[part],
            received,
            cut,
            kind,
        )

    pair = ring.scatter_first(step_of([(0, "none")], [])[0], cut)
    for step in range(ring.half - 1):
        how = ("low", "high") if step == 0 else ("full", "full")
        total = step_of([(2 * step + 1, how[0]), (2 * step + 2, how[1])], pair)
        pair = ring.scatter_next(total)
    (summed,) = step_of([(count - 1, "both")], pair, F32)
    attn_grad = summed[:rows, : 3 * GROUP].reshape(rows, 3, GROUP).transpose(1, 0, 2)
    out_grad = summed[:rows, 3 * GROUP :].T
    small = summed[rows_up : rows_up + 2].reshape(-1)[: smalls * columns]
    small = lax.dynamic_slice_in_dim(
        small.reshape(smalls, columns), tp * (columns // 4), columns // 4, 1
    )
    return (
        jnp.concatenate(outputs, axis=0),
        jnp.concatenate([b[0] for b in backward], axis=0),
        small[0:2],
        small[2:7],
        attn_grad,
        out_grad,
        small[7:],
        expert_grad[None, :D],
        expert_grad[2 * D : 2 * D + 1],
        expert_grad[None, D : 2 * D],
        expert_grad[2 * D + 1 : 2 * D + 2, :GROUP],
    )


def solution(mesh):
    both = ("wide", "tp")
    return jax.shard_map(
        functools.partial(body, mesh.shape["wide"]),
        mesh=mesh,
        in_specs=(
            P(both, None),
            P(None, both),
            P(None, both),
            P(None, "wide", "tp"),
            P("tp", "wide"),
            P(None, both),
            P("wide", None, "tp"),
            P("wide", "tp"),
            P("wide", None, "tp"),
            P("wide", "tp"),
            P("wide", None),
            P(both, None),
        ),
        out_specs=(
            P(both, None),
            P(both, None),
            P(None, both),
            P(None, both),
            P(None, "wide", "tp"),
            P("tp", "wide"),
            P(None, both),
            P("wide", None, "tp"),
            P("wide", "tp"),
            P("wide", None, "tp"),
            P("wide", "tp"),
        ),
        check_vma=False,
    )
```

time: 1600 us -> 457 us (0.29)
  blocking collectives: 528 us -> 0 us
  waiting for transfers between devices: 374 us -> 127 us
  local copies, waits for them, and re-layouts: 302 us -> 75.9 us
  other arithmetic: 213 us -> 14.2 us
  Pallas kernels: 0 us -> 157 us
  matrix products: 137 us -> 0.14 us
  starting transfers between devices: 17.2 us -> 60.4 us
    all_gather x5 -> x0, blocking collectives: 286 us -> none  [the longest x1 135 us: body(): lax.all_gather(router_weight, ('wide', 'tp'), axis=1, tiled=True)]
    all_to_all x3 -> x0, waiting for transfers between devices: 249 us -> none  [the longest x1 136 us: body(): lax.all_to_all(rows_all, 'wide', split_axis=0, concat_axis=1, tiled=True)]
    all_to_all x1 -> x0, blocking collectives: 165 us -> none  [body(): lax.all_to_all(slot_grads_all, 'wide', split_axis=0, concat_axis=1, tiled...]
    pallas_call x0 -> x35, Pallas kernels: none -> 157 us  [call(): pl.pallas_call(stripped, in_specs=list(specs) + [ANY] * waits, out_specs=...]
    dot_general x28 -> x1, matrix products: 133 us -> 0.14 us  [body(): rank = jnp.dot(is_chosen, lower)]
    ppermute x0 -> x60, waiting for transfers between devices: none -> 127 us  [the longest x24 75.4 us: backward(): return lax.ppermute(block, 'wide', self.behind)]
    convert_element_type x8 -> x6, local copies, waits for them, and re-layouts: 98.6 us -> 1.73 us  [the longest x1 1.36 us: body(): bias_grad.reshape(4, GROUP).astype(BF16)]
    reduce_scatter x4 -> x1, waiting for transfers between devices: 92.7 us -> 0.01 us  [body(): lax.psum_scatter(expert_grad.reshape(-1, D), 'tp', scatter_dimension=0, t...]
  transfers between devices with their start and end apart: 14 -> 62, of which waited for: 8 -> 26; matrix products, arithmetic and copies ran while one was open for 18% -> 7% of each run, Pallas kernels for 0% -> 26%
where the time goes in v1:
time: 457 us; the launch traced here: 451 us
  Pallas kernels  157 us (34%)
  waiting for transfers between devices  127 us (28%)
  local copies, waits for them, and re-layouts  75.9 us (17%)
  starting transfers between devices  60.4 us (13%)
  between operations  16.8 us (4%)
  other arithmetic  14.2 us (3%)
    pallas_call x35, Pallas kernels, call(): pl.pallas_call(stripped, in_specs=list(specs) + [ANY] * waits, out_specs=...  157 us
    ppermute x24, waiting for transfers between devices, backward(): return lax.ppermute(block, 'wide', self.behind)  75.4 us
    unnamed x248, local copies, waits for them, and re-layouts  51.3 us
    ppermute x6, waiting for transfers between devices, to_x(): return lax.ppermute(block, 'tp', [(i, i ^ 2) for i in range(4)])  29.8 us
    ppermute x24, starting transfers between devices, forward(): return lax.ppermute(block, 'wide', self.ahead)  28.4 us
    ppermute x24, starting transfers between devices, backward(): return lax.ppermute(block, 'wide', self.behind)  22.5 us
    ppermute x24, waiting for transfers between devices, forward(): return lax.ppermute(block, 'wide', self.ahead)  20 us
  transfers between devices with their start and end apart: 62, of which 26 were waited for; matrix products, arithmetic and copies ran while one was open for 7% of the time, Pallas kernels for 26%

profile of v1, /device:TPU:0, one launch (start us, length us, event | category | flops | bytes accessed | tf_op | source)
XLA Modules:
  0.0 451.4 jit_solution(4990994633055071910)
XLA Ops:
  10.6 2.7 collective-permute-start.1
  15.2 2.2 collective-permute-start.2
  17.4 3.6 collective-permute-done.2.refs_2_
  21.0 1.8 collective-permute-start.4
  24.4 2.0 collective-permute-done.4.refs_4_
  26.4 2.3 collective-permute-start.6
  29.5 2.8 collective-permute-done.6.refs_6_
  32.9 2.4 collective-permute-start.8
  36.9 4.3 collective-permute-done.9.refs_9_.refs_2_
  45.8 1.6 shard_map.203
  49.8 20.8 %collective-permute-done.11.refs_5_.refs_3_.refs_10_ = bf16[768,768]{1,0:T(8,128)(2,1)S(1)} collective-permute-done((bf16[768,768]{1,0:T(8,128)(2,1)}, bf16[768,768]{1,0:T(8,128)(2,1)S(1)}, u32[]{:S(2)}, u32[]{:S(2)}) %collective-permute-start.11) | collective-permute-done | bytes 1179680 | tf_op jit(solution)/shard_map/ppermute | solution.py:113
  70.6 1.6 shard_map.209
  80.8 1.8 collective-permute-start.13
  84.5 9.7 %collective-permute-done.15.refs_5_ = bf16[2,200,768]{2,1,0:T(8,128)(2,1)S(1)} collective-permute-done((bf16[2,200,768]{2,1,0:T(8,128)(2,1)S(1)}, bf16[2,200,768]{2,1,0:T(8,128)(2,1)S(1)}, u32[]{:S(2)}, u32[]{:S(2)}) %collective-permute-start.15) | collective-permute-done | bytes 614432 | tf_op jit(solution)/shard_map/ppermute | solution.py:91
  95.3 1.8 collective-permute-start.14
  98.0 10.3 %collective-permute-done.16.refs_8_.refs_7_ = bf16[2,200,768]{2,1,0:T(8,128)(2,1)} collective-permute-done((bf16[2,200,768]{2,1,0:T(8,128)(2,1)S(1)}, bf16[2,200,768]{2,1,0:T(8,128)(2,1)}, u32[]{:S(2)}, u32[]{:S(2)}) %collective-permute-start.16) | collective-permute-done | bytes 614432 | tf_op jit(solution)/shard_map/ppermute | solution.py:91
  110.0 2.1 collective-permute-start.17
  113.4 8.3 %shard_map.205 = (bf16[200,768]{1,0:T(8,128)(2,1)S(1)}, bf16[4,200,768]{2,1,0:T(8,128)(2,1)S(1)}, bf16[4,200,256]{2,1,0:T(8,128)(2,1)S(1)}, f32[200,128]{1,0:T(8...) custom-call(bf16[2,200,768]{2,1,0:T(8,128)(2,1)S(1)} %bitcast.85, ...), custom_call_target="tpu_custom_call" | custom-call | flops 6000000000 | bytes 9000000 | tf_op jit(solution)/shard_map/pallas_call | solution.py:504
  125.0 9.7 %shard_map.206 = (bf16[200,768]{1,0:T(8,128)(2,1)S(1)}, bf16[4,200,768]{2,1,0:T(8,128)(2,1)S(1)}, bf16[4,200,256]{2,1,0:T(8,128)(2,1)S(1)}, f32[200,128]{1,0:T(8...) custom-call(bf16[2,200,768]{2,1,0:T(8,128)(2,1)S(1)} %bitcast.86, ...), custom_call_target="tpu_custom_call" | custom-call | flops 6000000000 | bytes 9000000 | tf_op jit(solution)/shard_map/pallas_call | solution.py:504
  138.9 1.8 collective-permute-start.19
  141.1 14.7 %collective-permute-done.20.refs_5_ = bf16[2,200,768]{2,1,0:T(8,128)(2,1)} collective-permute-done((bf16[2,200,768]{2,1,0:T(8,128)(2,1)}, bf16[2,200,768]{2,1,0:T(8,128)(2,1)}, u32[]{:S(2)}, u32[]{:S(2)}) %collective-permute-start.20) | collective-permute-done | bytes 614432 | tf_op jit(solution)/shard_map/ppermute | solution.py:91
  156.1 1.8 collective-permute-start.21
  159.3 1.7 slice.302
  162.0 1.8 collective-permute-start.23
  166.5 1.7 collective-permute-done.22.refs_7_
  173.3 5.8 %shard_map.208 = (bf16[2656,768]{1,0:T(8,128)(2,1)}, bf16[2656,128]{1,0:T(8,128)(2,1)S(1)}) custom-call(s32[1]{0:T(128)S(6)} %convert_element_type.146.refs_0_, s32[11]{0:T(128)S(1)} %convert_element_type.147.refs_1_, s32[10,200]{1,0:T(8,128)S(1)} %fusion.14.refs_2_, bf16[2,200,768]{2,1,0:T(8,128)(2,1)S(1)} %shard_map.204.refs_3_.refs_1_, ...), custom_call_target="tpu_custom_call" | custom-call | flops 3000000000 | bytes 6000000 | tf_op jit(solution)/shard_map/pallas_call | solution.py:504
  180.0 2.3 shard_map.210
  183.8 5.9 %shard_map.207.refs_1_ = bf16[2656,768]{1,0:T(8,128)(2,1)} custom-call(s32[1]{0:T(128)S(6)} %convert_element_type.146.refs_0_, s32[11]{0:T(128)S(1)} %convert_element_type.147.refs_1_, s32[10,200]{1,0:T(8,128)S(1)} %fusion.14.refs_2_, bf16[2,200,768]{2,1,0:T(8,128)(2,1)} %get-tuple-element.115.refs_3_, bf16[2,200,768]{2,1,0:T(8,128)(2,1)} %collective-permute-done.19.refs_4_, ...), custom_call_target="tpu_custom_call" | custom-call | flops 3000000000 | bytes 6000000 | tf_op jit(solution)/shard_map/pallas_call | solution.py:504
  195.7 1.8 copy-done.76
  198.6 18.4 %shard_map.211 = (bf16[2656,3072]{1,0:T(8,128)(2,1)}, bf16[2656,3072]{1,0:T(8,128)(2,1)}, f32[2656,128]{1,0:T(8,128)S(1)}, bf16[2656,768]{1,0:T(8,128)(2,1)}, f3...) custom-call(s32[1]{0:T(128)S(6)} %convert_element_type.146.refs_0_, bf16[2656,768]{1,0:T(8,128)(2,1)} %shard_map.207.refs_1_, ...), custom_call_target="tpu_custom_call" | custom-call | flops 14000000000 | bytes 20000000 | tf_op jit(solution)/shard_map/pallas_call | solution.py:504
  217.8 2.7 shard_map.212.refs_1_
  222.1 13.0 %shard_map.213 = (bf16[1760,3072]{1,0:T(8,128)(2,1)}, bf16[1760,3072]{1,0:T(8,128)(2,1)}, f32[1760,128]{1,0:T(8,128)S(1)}, bf16[1760,768]{1,0:T(8,128)(2,1)S(1)}...) custom-call(s32[1]{0:T(128)S(6)} %convert_element_type.158.refs_0_, bf16[1760,768]{1,0:T(8,128)(2,1)} %copy-done.74, ...), custom_call_target="tpu_custom_call" | custom-call | flops 14000000000 | bytes 20000000 | tf_op jit(solution)/shard_map/pallas_call | solution.py:504
  236.8 2.2 shard_map.214
  247.4 5.0 %shard_map.217 = (bf16[2,200,768]{2,1,0:T(8,128)(2,1)S(1)}, bf16[2,200,768]{2,1,0:T(8,128)(2,1)S(1)}, bf16[2,200,768]{2,1,0:T(8,128)(2,1)S(1)}, bf16[2,200,768]{2,1,0:T(8,128)(2,1)S(1)}, bf16[2,200,768]{2,1,0:T(8,128)(2,1)S(1)}) custom-call(s32[1]{0:T(128)S(6)} %convert_element_type.146.refs_0_, s32[11]{0:T(128)S(1)} %copy-done.70, ...), custom_call_target="tpu_custom_call" | custom-call | flops 3000000000 | bytes 6000000 | tf_op jit(solution)/shard_map/pallas_call | solution.py:504
  255.4 1.6 collective-permute-start.31
  257.7 17.3 %shard_map.216 = (bf16[4,1552,768]{2,1,0:T(8,128)(2,1)}, bf16[2656,768]{1,0:T(8,128)(2,1)}) custom-call(s32[1]{0:T(128)S(6)} %convert_element_type.146.refs_0_, bf16[2656,768]{1,0:T(8,128)(2,1)} %shard_map.207.refs_1_, bf16[2656,768]{1,0:T(8,128)(2,1)} %get-tuple-element.117.refs_2_, bf16[2656,3072]{1,0:T(8,128)(2,1)} %get-tuple-element.120.refs_3_, ...), custom_call_target="tpu_custom_call" | custom-call | flops 14000000000 | bytes 30000000 | tf_op jit(solution)/shard_map/pallas_call | solution.py:504
  276.2 15.4 %shard_map.219 = (bf16[4,1552,768]{2,1,0:T(8,128)(2,1)}, bf16[1760,768]{1,0:T(8,128)(2,1)S(1)}) custom-call(s32[1]{0:T(128)S(6)} %convert_element_type.158.refs_0_, bf16[1760,768]{1,0:T(8,128)(2,1)} %copy-done.74, bf16[1760,768]{1,0:T(8,128)(2,1)} %copy-done.75, bf16[1760,3072]{1,0:T(8,128)(2,1)} %get-tuple-element.132.refs_3_, ...), custom_call_target="tpu_custom_call", output_to_operand_aliasing={{0}: (8, {})} | custom-call | flops 14000000000 | bytes 30000000 | tf_op jit(solution)/shard_map/pallas_call | solution.py:504
  294.5 1.6 collective-permute-start.33
  296.6 11.9 %collective-permute-done.33.refs_1_ = bf16[2,200,768]{2,1,0:T(8,128)(2,1)S(1)} collective-permute-done((bf16[2,200,768]{2,1,0:T(8,128)(2,1)}, bf16[2,200,768]{2,1,0:T(8,128)(2,1)S(1)}, u32[]{:S(2)}, u32[]{:S(2)}) %collective-permute-start.33) | collective-permute-done | bytes 614432 | tf_op jit(solution)/shard_map/ppermute | solution.py:91
  308.9 1.6 collective-permute-start.35
  311.0 1.9 copy-done.78
  312.9 2.2 shard_map.221
  315.1 5.1 %collective-permute-done.35.refs_1_.refs_3_ = bf16[2,200,768]{2,1,0:T(8,128)(2,1)S(1)} collective-permute-done((bf16[2,200,768]{2,1,0:T(8,128)(2,1)S(1)}, bf16[2,200,768]{2,1,0:T(8,128)(2,1)S(1)}, u32[]{:S(2)}, u32[]{:S(2)}) %collective-permute-start.35) | collective-permute-done | bytes 614432 | tf_op jit(solution)/shard_map/ppermute | solution.py:91
  321.2 1.6 collective-permute-start.37
  322.8 5.1 %shard_map.222 = (bf16[2,200,768]{2,1,0:T(8,128)(2,1)S(1)}, bf16[2,200,768]{2,1,0:T(8,128)(2,1)S(1)}, bf16[2,200,768]{2,1,0:T(8,128)(2,1)S(1)}, bf16[2,200,768]{2,1,0:T(8,128)(2,1)S(1)}, bf16[2,200,768]{2,1,0:T(8,128)(2,1)S(1)}) custom-call(s32[1]{0:T(128)S(6)} %convert_element_type.146.refs_0_, s32[11]{0:T(128)S(1)} %copy-done.71, ...), custom_call_target="tpu_custom_call" | custom-call | flops 3000000000 | bytes 6000000 | tf_op jit(solution)/shard_map/pallas_call | solution.py:504
  328.2 1.6 collective-permute-start.39
  330.7 10.0 %shard_map.227 = (f32[200,768]{1,0:T(8,128)S(1)}, bf16[200,768]{1,0:T(8,128)(2,1)S(1)}, bf16[4,200,768]{2,1,0:T(8,128)(2,1)S(1)}, f32[8,768]{1,0:T(8,128)S(1)}, f32[4,768]{1,0:T(4,128)S(1)}) custom-call(bf16[2,200,768]{2,1,0:T(8,128)(2,1)S(1)} %bitcast.87, bf16[2,200,768]{2,1,0:T(8,128)(2,1)S(1)} %shard_map.204.refs_3_.refs_1_, ...), custom_call_target="tpu_custom_call" | custom-call | flops 8000000000 | bytes 9000000 | tf_op jit(solution)/shard_map/pallas_call | solution.py:504
  343.6 10.3 %shard_map.228 = (f32[200,768]{1,0:T(8,128)S(1)}, bf16[200,768]{1,0:T(8,128)(2,1)S(1)}, bf16[4,200,768]{2,1,0:T(8,128)(2,1)S(1)}, f32[8,768]{1,0:T(8,128)S(1)}, f32[4,768]{1,0:T(4,128)S(1)}) custom-call(bf16[2,200,768]{2,1,0:T(8,128)(2,1)S(1)} %bitcast.88, bf16[2,200,768]{2,1,0:T(8,128)(2,1)S(1)} %shard_map.204.refs_3_.refs_1_, ...), custom_call_target="tpu_custom_call" | custom-call | flops 8000000000 | bytes 9000000 | tf_op jit(solution)/shard_map/pallas_call | solution.py:504
  354.8 4.0 shard_map.229
  361.6 4.0 shard_map.230
  365.9 10.2 %collective-permute-done.41.refs_1_ = bf16[2,200,768]{2,1,0:T(8,128)(2,1)} collective-permute-done((bf16[2,200,768]{2,1,0:T(8,128)(2,1)}, bf16[2,200,768]{2,1,0:T(8,128)(2,1)}, u32[]{:S(2)}, u32[]{:S(2)}) %collective-permute-start.41) | collective-permute-done | bytes 614432 | tf_op jit(solution)/shard_map/ppermute | solution.py:91
  378.5 2.4 shard_map.226
  383.0 2.2 shard_map.232
  389.7 8.4 %collective-permute-done.46 = f32[15,768]{1,0:T(8,128)S(1)} collective-permute-done((f32[15,768]{1,0:T(8,128)S(1)}, f32[15,768]{1,0:T(8,128)S(1)}, u32[]{:S(2)}, u32[]{:S(2)}) %collective-permute-start.46) | collective-permute-done | bytes 46112 | tf_op jit(solution)/shard_map/ppermute | solution.py:113
  401.5 1.6 collective-permute-start.52
  403.5 3.9 collective-permute-done.53.refs_5_
  408.8 1.6 collective-permute-start.54
  412.5 1.9 collective-permute-done.54.refs_4_
  417.1 1.9 collective-permute-start.56
  420.7 3.1 collective-permute-done.56.refs_4_
  423.8 2.2 collective-permute-done.57.refs_5_
  429.8 2.3 collective-permute-done.58.refs_4_
  437.3 2.0 convert_element_type.169
  439.4 2.5 slice_bitcast_fusion
  (474 shorter events, 120.8 us)
Async XLA Ops:
  7.2 187.6 %all-gather.2.cloned.1.call-start = ((), (), s32[]{:S(2)}) async-start(), calls=%async_computation.1 | async-start | bytes 11919360 | tf_op jit(solution)/shard_map/all_gather | solution.py:815
  9.1 1.4 collective-permute-start
  10.6 4.3 collective-permute-start.1
  15.2 5.8 %collective-permute-start.2 = (bf16[112,768]{1,0:T(8,128)(2,1)S(1)}, bf16[112,768]{1,0:T(8,128)(2,1)S(1)}, u32[]{:S(2)}, u32[]{:S(2)}) collective-permute-start(bf16[112,768]{1,0:T(8,128)(2,1)S(1)} %fusion.8.refs_1_), channel_id=1, source_target_pairs={{0,8},{8,16},{16,24},{24,28},{28,20},{20,12},{12,4},{4,0},{1,9},{9... | collective-permute-start | bytes 516104 | tf_op jit(solution)/shard_map/ppermute | solution.py:88
  17.4 6.1 %collective-permute-start.3 = (bf16[112,768]{1,0:T(8,128)(2,1)S(1)}, bf16[112,768]{1,0:T(8,128)(2,1)S(1)}, u32[]{:S(2)}, u32[]{:S(2)}) collective-permute-start(bf16[112,768]{1,0:T(8,128)(2,1)S(1)} %fusion.8.refs_1_), channel_id=1, source_target_pairs={{0,4},{8,0},{16,8},{24,16},{28,24},{20,28},{12,20},{4,12},{1,5},{9... | collective-permute-start | bytes 516104 | tf_op jit(solution)/shard_map/ppermute | solution.py:91
  21.0 5.4 %collective-permute-start.4 = (bf16[112,768]{1,0:T(8,128)(2,1)S(1)}, bf16[112,768]{1,0:T(8,128)(2,1)S(1)}, u32[]{:S(2)}, u32[]{:S(2)}) collective-permute-start(bf16[112,768]{1,0:T(8,128)(2,1)S(1)} %collective-permute-done.2.refs_2_), channel_id=1, source_target_pairs={{0,8},{8,16},{16,24},{24,28},{28,20},{20,12},{12,4},{4,0},{1,9},{9... | collective-permute-start | bytes 516104 | tf_op jit(solution)/shard_map/ppermute | solution.py:88
  23.5 6.0 %collective-permute-start.5 = (bf16[112,768]{1,0:T(8,128)(2,1)S(1)}, bf16[112,768]{1,0:T(8,128)(2,1)S(1)}, u32[]{:S(2)}, u32[]{:S(2)}) collective-permute-start(bf16[112,768]{1,0:T(8,128)(2,1)S(1)} %collective-permute-done.3.refs_3_), channel_id=1, source_target_pairs={{0,4},{8,0},{16,8},{24,16},{28,24},{20,28},{12,20},{4,12},{1,5},{9... | collective-permute-start | bytes 516104 | tf_op jit(solution)/shard_map/ppermute | solution.py:91
  26.4 5.9 %collective-permute-start.6 = (bf16[112,768]{1,0:T(8,128)(2,1)S(1)}, bf16[112,768]{1,0:T(8,128)(2,1)S(1)}, u32[]{:S(2)}, u32[]{:S(2)}) collective-permute-start(bf16[112,768]{1,0:T(8,128)(2,1)S(1)} %collective-permute-done.4.refs_4_), channel_id=1, source_target_pairs={{0,8},{8,16},{16,24},{24,28},{28,20},{20,12},{12,4},{4,0},{1,9},{9... | collective-permute-start | bytes 516104 | tf_op jit(solution)/shard_map/ppermute | solution.py:88
  29.5 5.9 %collective-permute-start.7 = (bf16[112,768]{1,0:T(8,128)(2,1)S(1)}, bf16[112,768]{1,0:T(8,128)(2,1)S(1)}, u32[]{:S(2)}, u32[]{:S(2)}) collective-permute-start(bf16[112,768]{1,0:T(8,128)(2,1)S(1)} %collective-permute-done.5.refs_5_), channel_id=1, source_target_pairs={{0,4},{8,0},{16,8},{24,16},{28,24},{20,28},{12,20},{4,12},{1,5},{9... | collective-permute-start | bytes 516104 | tf_op jit(solution)/shard_map/ppermute | solution.py:91
  32.9 8.3 %collective-permute-start.8 = (bf16[64,768]{1,0:T(8,128)(2,1)}, bf16[64,768]{1,0:T(8,128)(2,1)S(1)}, u32[]{:S(2)}, u32[]{:S(2)}) collective-permute-start(bf16[64,768]{1,0:T(8,128)(2,1)} %slice.281), channel_id=1, source_target_pairs={{0,8},{8,16},{16,24},{24,28},{28,20},{20,12},{12,4},{4,0},{1,9},{9... | collective-permute-start | bytes 294920 | tf_op jit(solution)/shard_map/ppermute | solution.py:88
  36.6 4.6 %collective-permute-start.9 = (bf16[48,768]{1,0:T(8,128)(2,1)}, bf16[48,768]{1,0:T(8,128)(2,1)S(1)}, u32[]{:S(2)}, u32[]{:S(2)}) collective-permute-start(bf16[48,768]{1,0:T(8,128)(2,1)} %slice.282), channel_id=1, source_target_pairs={{0,4},{8,0},{16,8},{24,16},{28,24},{20,28},{12,20},{4,12},{1,5},{9... | collective-permute-start | bytes 221192 | tf_op jit(solution)/shard_map/ppermute | solution.py:91
  48.1 22.5 %collective-permute-start.11 = (bf16[768,768]{1,0:T(8,128)(2,1)}, bf16[768,768]{1,0:T(8,128)(2,1)S(1)}, u32[]{:S(2)}, u32[]{:S(2)}) collective-permute-start(bf16[768,768]{1,0:T(8,128)(2,1)} %bitcast.15.refs_3_.refs_8_), channel_id=1, source_target_pairs={{0,2},{1,3},{2,0},{3,1},{4,6},{5,7},{6,4},{7,5},{8,10},{9,11},{10,... | collective-permute-start | bytes 3538952 | tf_op jit(solution)/shard_map/ppermute | solution.py:113
  73.3 364.1 %reduce-scatter.2.cloned.1.call-start = ((), (), s32[]{:S(2)}) async-start(), calls=%async_computation.2 | async-start | bytes 11919360 | tf_op jit(solution)/shard_map/reduce_scatter | solution.py:931
  80.5 13.7 %collective-permute-start.15 = (bf16[2,200,768]{2,1,0:T(8,128)(2,1)S(1)}, bf16[2,200,768]{2,1,0:T(8,128)(2,1)S(1)}, u32[]{:S(2)}, u32[]{:S(2)}) collective-permute-start(bf16[2,200,768]{2,1,0:T(8,128)(2,1)S(1)} %shard_map.204.refs_3_.refs_1_), channel_id=1, source_target_pairs={{0,4},{8,0},{16,8},{24,16},{28,24},{20,28},{12,20},{4,12},{1,5},{9... | collective-permute-start | bytes 1843208 | tf_op jit(solution)/shard_map/ppermute | solution.py:91
  80.8 14.4 %collective-permute-start.13 = (bf16[2,200,768]{2,1,0:T(8,128)(2,1)S(1)}, bf16[2,200,768]{2,1,0:T(8,128)(2,1)S(1)}, u32[]{:S(2)}, u32[]{:S(2)}) collective-permute-start(bf16[2,200,768]{2,1,0:T(8,128)(2,1)S(1)} %shard_map.204.refs_3_.refs_1_), channel_id=1, source_target_pairs={{0,8},{8,16},{16,24},{24,28},{28,20},{20,12},{12,4},{4,0},{1,9},{9... | collective-permute-start | bytes 1843208 | tf_op jit(solution)/shard_map/ppermute | solution.py:88
  82.6 29.7 %collective-permute-start.10 = (bf16[768,768]{1,0:T(8,128)(2,1)}, bf16[768,768]{1,0:T(8,128)(2,1)}, u32[]{:S(2)}, u32[]{:S(2)}) collective-permute-start(bf16[768,768]{1,0:T(8,128)(2,1)} %bitcast.15.refs_3_.refs_8_), channel_id=1, source_target_pairs={{0,1},{1,0},{2,3},{3,2},{4,5},{5,4},{6,7},{7,6},{8,9},{9,8},{10,11... | collective-permute-start | bytes 3538952 | tf_op jit(solution)/shard_map/ppermute | solution.py:109
  83.6 28.7 %collective-permute-start.12 = (bf16[768,768]{1,0:T(8,128)(2,1)S(1)}, bf16[768,768]{1,0:T(8,128)(2,1)}, u32[]{:S(2)}, u32[]{:S(2)}) collective-permute-start(bf16[768,768]{1,0:T(8,128)(2,1)S(1)} %copy-done.5), channel_id=1, source_target_pairs={{0,1},{1,0},{2,3},{3,2},{4,5},{5,4},{6,7},{7,6},{8,9},{9,8},{10,11... | collective-permute-start | bytes 3538952 | tf_op jit(solution)/shard_map/ppermute | solution.py:109
  94.1 14.2 %collective-permute-start.16 = (bf16[2,200,768]{2,1,0:T(8,128)(2,1)S(1)}, bf16[2,200,768]{2,1,0:T(8,128)(2,1)}, u32[]{:S(2)}, u32[]{:S(2)}) collective-permute-start(bf16[2,200,768]{2,1,0:T(8,128)(2,1)S(1)} %collective-permute-done.15.refs_5_), channel_id=1, source_target_pairs={{0,4},{8,0},{16,8},{24,16},{28,24},{20,28},{12,20},{4,12},{1,5},{9... | collective-permute-start | bytes 1843208 | tf_op jit(solution)/shard_map/ppermute | solution.py:91
  95.3 14.8 %collective-permute-start.14 = (bf16[2,200,768]{2,1,0:T(8,128)(2,1)S(1)}, bf16[2,200,768]{2,1,0:T(8,128)(2,1)}, u32[]{:S(2)}, u32[]{:S(2)}) collective-permute-start(bf16[2,200,768]{2,1,0:T(8,128)(2,1)S(1)} %collective-permute-done.13.refs_4_), channel_id=1, source_target_pairs={{0,8},{8,16},{16,24},{24,28},{28,20},{20,12},{12,4},{4,0},{1,9},{9... | collective-permute-start | bytes 1843208 | tf_op jit(solution)/shard_map/ppermute | solution.py:88
  108.3 16.5 %collective-permute-start.18 = (bf16[2,200,768]{2,1,0:T(8,128)(2,1)}, bf16[2,200,768]{2,1,0:T(8,128)(2,1)S(1)}, u32[]{:S(2)}, u32[]{:S(2)}) collective-permute-start(bf16[2,200,768]{2,1,0:T(8,128)(2,1)} %collective-permute-done.16.refs_8_.refs_7_), channel_id=1, source_target_pairs={{0,4},{8,0},{16,8},{24,16},{28,24},{20,28},{12,20},{4,12},{1,5},{9... | collective-permute-start | bytes 1843208 | tf_op jit(solution)/shard_map/ppermute | solution.py:91
  110.0 14.9 %collective-permute-start.17 = (bf16[2,200,768]{2,1,0:T(8,128)(2,1)}, bf16[2,200,768]{2,1,0:T(8,128)(2,1)S(1)}, u32[]{:S(2)}, u32[]{:S(2)}) collective-permute-start(bf16[2,200,768]{2,1,0:T(8,128)(2,1)} %collective-permute-done.14.refs_7_.refs_6_), channel_id=1, source_target_pairs={{0,8},{8,16},{16,24},{24,28},{28,20},{20,12},{12,4},{4,0},{1,9},{9... | collective-permute-start | bytes 1843208 | tf_op jit(solution)/shard_map/ppermute | solution.py:88
  138.7 17.1 %collective-permute-start.20 = (bf16[2,200,768]{2,1,0:T(8,128)(2,1)}, bf16[2,200,768]{2,1,0:T(8,128)(2,1)}, u32[]{:S(2)}, u32[]{:S(2)}) collective-permute-start(bf16[2,200,768]{2,1,0:T(8,128)(2,1)} %get-tuple-element.115.refs_3_), channel_id=1, source_target_pairs={{0,4},{8,0},{16,8},{24,16},{28,24},{20,28},{12,20},{4,12},{1,5},{9... | collective-permute-start | bytes 1843208 | tf_op jit(solution)/shard_map/ppermute | solution.py:91
  138.9 17.1 %collective-permute-start.19 = (bf16[2,200,768]{2,1,0:T(8,128)(2,1)}, bf16[2,200,768]{2,1,0:T(8,128)(2,1)}, u32[]{:S(2)}, u32[]{:S(2)}) collective-permute-start(bf16[2,200,768]{2,1,0:T(8,128)(2,1)} %get-tuple-element.115.refs_3_), channel_id=1, source_target_pairs={{0,8},{8,16},{16,24},{24,28},{28,20},{20,12},{12,4},{4,0},{1,9},{9... | collective-permute-start | bytes 1843208 | tf_op jit(solution)/shard_map/ppermute | solution.py:88
  155.8 12.3 %collective-permute-start.22 = (bf16[2,200,768]{2,1,0:T(8,128)(2,1)}, bf16[2,200,768]{2,1,0:T(8,128)(2,1)}, u32[]{:S(2)}, u32[]{:S(2)}) collective-permute-start(bf16[2,200,768]{2,1,0:T(8,128)(2,1)} %collective-permute-done.20.refs_5_), channel_id=1, source_target_pairs={{0,4},{8,0},{16,8},{24,16},{28,24},{20,28},{12,20},{4,12},{1,5},{9... | collective-permute-start | bytes 1843208 | tf_op jit(solution)/shard_map/ppermute | solution.py:91
  156.1 13.6 %collective-permute-start.21 = (bf16[2,200,768]{2,1,0:T(8,128)(2,1)}, bf16[2,200,768]{2,1,0:T(8,128)(2,1)}, u32[]{:S(2)}, u32[]{:S(2)}) collective-permute-start(bf16[2,200,768]{2,1,0:T(8,128)(2,1)} %collective-permute-done.19.refs_4_), channel_id=1, source_target_pairs={{0,8},{8,16},{16,24},{24,28},{28,20},{20,12},{12,4},{4,0},{1,9},{9... | collective-permute-start | bytes 1843208 | tf_op jit(solution)/shard_map/ppermute | solution.py:88
  161.0 18.9 %collective-permute-start.24 = (bf16[1,200,768]{2,1,0:T(8,128)(2,1)}, bf16[1,200,768]{2,1,0:T(8,128)(2,1)S(1)}, u32[]{:S(2)}, u32[]{:S(2)}) collective-permute-start(bf16[1,200,768]{2,1,0:T(8,128)(2,1)} %slice.302), channel_id=1, source_target_pairs={{0,4},{8,0},{16,8},{24,16},{28,24},{20,28},{12,20},{4,12},{1,5},{9... | collective-permute-start | bytes 921608 | tf_op jit(solution)/shard_map/ppermute | solution.py:91
  162.0 18.0 %collective-permute-start.23 = (bf16[1,200,768]{2,1,0:T(8,128)(2,1)}, bf16[1,200,768]{2,1,0:T(8,128)(2,1)}, u32[]{:S(2)}, u32[]{:S(2)}) collective-permute-start(bf16[1,200,768]{2,1,0:T(8,128)(2,1)} %slice.301), channel_id=1, source_target_pairs={{0,8},{8,16},{16,24},{24,28},{28,20},{20,12},{12,4},{4,0},{1,9},{9... | collective-permute-start | bytes 921608 | tf_op jit(solution)/shard_map/ppermute | solution.py:88
  163.8 73.0 %copy-start.54 = (s32[6,200]{1,0:T(8,128)}, s32[6,200]{1,0:T(8,128)S(1)}, u32[]{:S(2)}) copy-start(s32[6,200]{1,0:T(8,128)S(1)} %fusion.17.refs_2_) | copy-start | bytes 14404
  165.0 71.8 %copy-start.72 = (s32[7]{0:T(128)}, s32[7]{0:T(128)S(1)}, u32[]{:S(2)}) copy-start(s32[7]{0:T(128)S(1)} %convert_element_type.159.refs_1_) | copy-start | bytes 88
  168.1 21.5 %collective-permute-start.26 = (bf16[2,200,768]{2,1,0:T(8,128)(2,1)}, bf16[2,200,768]{2,1,0:T(8,128)(2,1)S(1)}, u32[]{:S(2)}, u32[]{:S(2)}) collective-permute-start(bf16[2,200,768]{2,1,0:T(8,128)(2,1)} %collective-permute-done.22.refs_7_), channel_id=1, source_target_pairs={{0,4},{8,0},{16,8},{24,16},{28,24},{20,28},{12,20},{4,12},{1,5},{9... | collective-permute-start | bytes 1843208 | tf_op jit(solution)/shard_map/ppermute | solution.py:91
  169.7 23.2 %collective-permute-start.25 = (bf16[2,200,768]{2,1,0:T(8,128)(2,1)}, bf16[2,200,768]{2,1,0:T(8,128)(2,1)S(1)}, u32[]{:S(2)}, u32[]{:S(2)}) collective-permute-start(bf16[2,200,768]{2,1,0:T(8,128)(2,1)} %collective-permute-done.21.refs_6_), channel_id=1, source_target_pairs={{0,8},{8,16},{16,24},{24,28},{28,20},{20,12},{12,4},{4,0},{1,9},{9... | collective-permute-start | bytes 1843208 | tf_op jit(solution)/shard_map/ppermute | solution.py:88
  191.3 26.5 %collective-permute-start.28 = (bf16[1,200,768]{2,1,0:T(8,128)(2,1)}, bf16[1,200,768]{2,1,0:T(8,128)(2,1)}, u32[]{:S(2)}, u32[]{:S(2)}) collective-permute-start(bf16[1,200,768]{2,1,0:T(8,128)(2,1)} %slice.304), channel_id=1, source_target_pairs={{0,4},{8,0},{16,8},{24,16},{28,24},{20,28},{12,20},{4,12},{1,5},{9... | collective-permute-start | bytes 921608 | tf_op jit(solution)/shard_map/ppermute | solution.py:91
  194.4 23.3 %collective-permute-start.27 = (bf16[1,200,768]{2,1,0:T(8,128)(2,1)}, bf16[1,200,768]{2,1,0:T(8,128)(2,1)}, u32[]{:S(2)}, u32[]{:S(2)}) collective-permute-start(bf16[1,200,768]{2,1,0:T(8,128)(2,1)} %slice.303), channel_id=1, source_target_pairs={{0,8},{8,16},{16,24},{24,28},{28,20},{20,12},{12,4},{4,0},{1,9},{9... | collective-permute-start | bytes 921608 | tf_op jit(solution)/shard_map/ppermute | solution.py:88
  241.6 12.4 %collective-permute-start.30 = (bf16[1,200,768]{2,1,0:T(8,128)(2,1)}, bf16[1,200,768]{2,1,0:T(8,128)(2,1)S(1)}, u32[]{:S(2)}, u32[]{:S(2)}) collective-permute-start(bf16[1,200,768]{2,1,0:T(8,128)(2,1)} %get-tuple-element.242), channel_id=1, source_target_pairs={{0,8},{8,16},{16,24},{24,28},{28,20},{20,12},{12,4},{4,0},{1,9},{9... | collective-permute-start | bytes 921608 | tf_op jit(solution)/shard_map/ppermute | solution.py:88
  243.1 11.0 %collective-permute-start.29 = (bf16[1,200,768]{2,1,0:T(8,128)(2,1)}, bf16[1,200,768]{2,1,0:T(8,128)(2,1)}, u32[]{:S(2)}, u32[]{:S(2)}) collective-permute-start(bf16[1,200,768]{2,1,0:T(8,128)(2,1)} %get-tuple-element.243), channel_id=1, source_target_pairs={{0,4},{8,0},{16,8},{24,16},{28,24},{20,28},{12,20},{4,12},{1,5},{9... | collective-permute-start | bytes 921608 | tf_op jit(solution)/shard_map/ppermute | solution.py:91
  255.4 19.6 %collective-permute-start.31 = (bf16[2,200,768]{2,1,0:T(8,128)(2,1)S(1)}, bf16[2,200,768]{2,1,0:T(8,128)(2,1)S(1)}, u32[]{:S(2)}, u32[]{:S(2)}) collective-permute-start(bf16[2,200,768]{2,1,0:T(8,128)(2,1)S(1)} %get-tuple-element.129.refs_8_), channel_id=1, source_target_pairs={{0,4},{8,0},{16,8},{24,16},{28,24},{20,28},{12,20},{4,12},{1,5},{9... | collective-permute-start | bytes 1843208 | tf_op jit(solution)/shard_map/ppermute | solution.py:91
  257.0 18.0 %collective-permute-start.32 = (bf16[2,200,768]{2,1,0:T(8,128)(2,1)S(1)}, bf16[2,200,768]{2,1,0:T(8,128)(2,1)S(1)}, u32[]{:S(2)}, u32[]{:S(2)}) collective-permute-start(bf16[2,200,768]{2,1,0:T(8,128)(2,1)S(1)} %get-tuple-element.130.refs_9_), channel_id=1, source_target_pairs={{0,8},{8,16},{16,24},{24,28},{28,20},{20,12},{12,4},{4,0},{1,9},{9... | collective-permute-start | bytes 1843208 | tf_op jit(solution)/shard_map/ppermute | solution.py:88
  294.5 14.0 %collective-permute-start.33 = (bf16[2,200,768]{2,1,0:T(8,128)(2,1)}, bf16[2,200,768]{2,1,0:T(8,128)(2,1)S(1)}, u32[]{:S(2)}, u32[]{:S(2)}) collective-permute-start(bf16[2,200,768]{2,1,0:T(8,128)(2,1)} %copy-done.66), channel_id=1, source_target_pairs={{0,4},{8,0},{16,8},{24,16},{28,24},{20,28},{12,20},{4,12},{1,5},{9... | collective-permute-start | bytes 1843208 | tf_op jit(solution)/shard_map/ppermute | solution.py:91
  296.1 12.4 %collective-permute-start.34 = (bf16[2,200,768]{2,1,0:T(8,128)(2,1)}, bf16[2,200,768]{2,1,0:T(8,128)(2,1)S(1)}, u32[]{:S(2)}, u32[]{:S(2)}) collective-permute-start(bf16[2,200,768]{2,1,0:T(8,128)(2,1)} %copy-done.65), channel_id=1, source_target_pairs={{0,8},{8,16},{16,24},{24,28},{28,20},{20,12},{12,4},{4,0},{1,9},{9... | collective-permute-start | bytes 1843208 | tf_op jit(solution)/shard_map/ppermute | solution.py:88
  308.9 11.3 %collective-permute-start.35 = (bf16[2,200,768]{2,1,0:T(8,128)(2,1)S(1)}, bf16[2,200,768]{2,1,0:T(8,128)(2,1)S(1)}, u32[]{:S(2)}, u32[]{:S(2)}) collective-permute-start(bf16[2,200,768]{2,1,0:T(8,128)(2,1)S(1)} %get-tuple-element.143.refs_4_), channel_id=1, source_target_pairs={{0,4},{8,0},{16,8},{24,16},{28,24},{20,28},{12,20},{4,12},{1,5},{9... | collective-permute-start | bytes 1843208 | tf_op jit(solution)/shard_map/ppermute | solution.py:91
  310.5 10.1 %collective-permute-start.36 = (bf16[2,200,768]{2,1,0:T(8,128)(2,1)S(1)}, bf16[2,200,768]{2,1,0:T(8,128)(2,1)S(1)}, u32[]{:S(2)}, u32[]{:S(2)}) collective-permute-start(bf16[2,200,768]{2,1,0:T(8,128)(2,1)S(1)} %get-tuple-element.144.refs_5_), channel_id=1, source_target_pairs={{0,8},{8,16},{16,24},{24,28},{28,20},{20,12},{12,4},{4,0},{1,9},{9... | collective-permute-start | bytes 1843208 | tf_op jit(solution)/shard_map/ppermute | solution.py:88
  320.7 7.2 %collective-permute-start.38 = (bf16[1,200,768]{2,1,0:T(8,128)(2,1)S(1)}, bf16[1,200,768]{2,1,0:T(8,128)(2,1)S(1)}, u32[]{:S(2)}, u32[]{:S(2)}) collective-permute-start(bf16[1,200,768]{2,1,0:T(8,128)(2,1)S(1)} %get-tuple-element.240), channel_id=1, source_target_pairs={{0,8},{8,16},{16,24},{24,28},{28,20},{20,12},{12,4},{4,0},{1,9},{9... | collective-permute-start | bytes 921608 | tf_op jit(solution)/shard_map/ppermute | solution.py:88
  321.2 6.9 %collective-permute-start.37 = (bf16[1,200,768]{2,1,0:T(8,128)(2,1)S(1)}, bf16[1,200,768]{2,1,0:T(8,128)(2,1)S(1)}, u32[]{:S(2)}, u32[]{:S(2)}) collective-permute-start(bf16[1,200,768]{2,1,0:T(8,128)(2,1)S(1)} %get-tuple-element.241), channel_id=1, source_target_pairs={{0,4},{8,0},{16,8},{24,16},{28,24},{20,28},{12,20},{4,12},{1,5},{9... | collective-permute-start | bytes 921608 | tf_op jit(solution)/shard_map/ppermute | solution.py:91
  328.2 13.4 %collective-permute-start.39 = (bf16[2,200,768]{2,1,0:T(8,128)(2,1)S(1)}, bf16[2,200,768]{2,1,0:T(8,128)(2,1)S(1)}, u32[]{:S(2)}, u32[]{:S(2)}) collective-permute-start(bf16[2,200,768]{2,1,0:T(8,128)(2,1)S(1)} %get-tuple-element.151.refs_13_), channel_id=1, source_target_pairs={{0,4},{8,0},{16,8},{24,16},{28,24},{20,28},{12,20},{4,12},{1,5},{9... | collective-permute-start | bytes 1843208 | tf_op jit(solution)/shard_map/ppermute | solution.py:91
  329.8 11.8 %collective-permute-start.40 = (bf16[2,200,768]{2,1,0:T(8,128)(2,1)S(1)}, bf16[2,200,768]{2,1,0:T(8,128)(2,1)S(1)}, u32[]{:S(2)}, u32[]{:S(2)}) collective-permute-start(bf16[2,200,768]{2,1,0:T(8,128)(2,1)S(1)} %get-tuple-element.153.refs_14_), channel_id=1, source_target_pairs={{0,8},{8,16},{16,24},{24,28},{28,20},{20,12},{12,4},{4,0},{1,9},{9... | collective-permute-start | bytes 1843208 | tf_op jit(solution)/shard_map/ppermute | solution.py:88
  358.8 24.2 %collective-permute-start.48 = (bf16[8,96,768]{2,1,0:T(8,128)(2,1)}, bf16[8,96,768]{2,1,0:T(8,128)(2,1)}, u32[]{:S(2)}, u32[]{:S(2)}) collective-permute-start(bf16[8,96,768]{2,1,0:T(8,128)(2,1)} %get-tuple-element.184), channel_id=1, source_target_pairs={{0,1},{1,0},{2,3},{3,2},{4,5},{5,4},{6,7},{7,6},{8,9},{9,8},{10,11... | collective-permute-start | bytes 3538952 | tf_op jit(solution)/shard_map/ppermute | solution.py:109
  359.6 16.5 %collective-permute-start.41 = (bf16[2,200,768]{2,1,0:T(8,128)(2,1)}, bf16[2,200,768]{2,1,0:T(8,128)(2,1)}, u32[]{:S(2)}, u32[]{:S(2)}) collective-permute-start(bf16[2,200,768]{2,1,0:T(8,128)(2,1)} %get-tuple-element.154.refs_13_), channel_id=1, source_target_pairs={{0,4},{8,0},{16,8},{24,16},{28,24},{20,28},{12,20},{4,12},{1,5},{9... | collective-permute-start | bytes 1843208 | tf_op jit(solution)/shard_map/ppermute | solution.py:91
  361.2 16.2 %collective-permute-start.42 = (bf16[2,200,768]{2,1,0:T(8,128)(2,1)}, bf16[2,200,768]{2,1,0:T(8,128)(2,1)}, u32[]{:S(2)}, u32[]{:S(2)}) collective-permute-start(bf16[2,200,768]{2,1,0:T(8,128)(2,1)} %get-tuple-element.156.refs_14_), channel_id=1, source_target_pairs={{0,8},{8,16},{16,24},{24,28},{28,20},{20,12},{12,4},{4,0},{1,9},{9... | collective-permute-start | bytes 1843208 | tf_op jit(solution)/shard_map/ppermute | solution.py:88
  365.6 34.2 %collective-permute-start.47 = (bf16[8,96,768]{2,1,0:T(8,128)(2,1)}, bf16[8,96,768]{2,1,0:T(8,128)(2,1)S(1)}, u32[]{:S(2)}, u32[]{:S(2)}) collective-permute-start(bf16[8,96,768]{2,1,0:T(8,128)(2,1)} %get-tuple-element.182), channel_id=1, source_target_pairs={{0,1},{1,0},{2,3},{3,2},{4,5},{5,4},{6,7},{7,6},{8,9},{9,8},{10,11... | collective-permute-start | bytes 3538952 | tf_op jit(solution)/shard_map/ppermute | solution.py:109
  381.0 38.2 %collective-permute-start.43 = (bf16[2,200,768]{2,1,0:T(8,128)(2,1)}, bf16[2,200,768]{2,1,0:T(8,128)(2,1)}, u32[]{:S(2)}, u32[]{:S(2)}) collective-permute-start(bf16[2,200,768]{2,1,0:T(8,128)(2,1)} %get-tuple-element.157), channel_id=1, source_target_pairs={{0,4},{8,0},{16,8},{24,16},{28,24},{20,28},{12,20},{4,12},{1,5},{9... | collective-permute-start | bytes 1843208 | tf_op jit(solution)/shard_map/ppermute | solution.py:91
  382.5 36.6 %collective-permute-start.44 = (bf16[2,200,768]{2,1,0:T(8,128)(2,1)}, bf16[2,200,768]{2,1,0:T(8,128)(2,1)}, u32[]{:S(2)}, u32[]{:S(2)}) collective-permute-start(bf16[2,200,768]{2,1,0:T(8,128)(2,1)} %get-tuple-element.158), channel_id=1, source_target_pairs={{0,8},{8,16},{16,24},{24,28},{28,20},{20,12},{12,4},{4,0},{1,9},{9... | collective-permute-start | bytes 1843208 | tf_op jit(solution)/shard_map/ppermute | solution.py:88
  386.0 14.9 %collective-permute-start.51 = (bf16[3,96,768]{2,1,0:T(8,128)(2,1)}, bf16[3,96,768]{2,1,0:T(8,128)(2,1)S(1)}, u32[]{:S(2)}, u32[]{:S(2)}) collective-permute-start(bf16[3,96,768]{2,1,0:T(8,128)(2,1)} %get-tuple-element.189), channel_id=1, source_target_pairs={{0,2},{1,3},{2,0},{3,1},{4,6},{5,7},{6,4},{7,5},{8,10},{9,11},{10,... | collective-permute-start | bytes 1327112 | tf_op jit(solution)/shard_map/ppermute | solution.py:113
  387.8 1.3 collective-permute-start.45
  389.1 9.0 %collective-permute-start.46 = (f32[15,768]{1,0:T(8,128)S(1)}, f32[15,768]{1,0:T(8,128)S(1)}, u32[]{:S(2)}, u32[]{:S(2)}) collective-permute-start(f32[15,768]{1,0:T(8,128)S(1)} %add.179), channel_id=1, source_target_pairs={{0,2},{1,3},{2,0},{3,1},{4,6},{5,7},{6,4},{7,5},{8,10},{9,11},{10,... | collective-permute-start | bytes 138248 | tf_op jit(solution)/shard_map/ppermute | solution.py:113
  398.1 12.7 %collective-permute-start.50 = (bf16[2,96,768]{2,1,0:T(8,128)(2,1)}, bf16[2,96,768]{2,1,0:T(8,128)(2,1)}, u32[]{:S(2)}, u32[]{:S(2)}) collective-permute-start(bf16[2,96,768]{2,1,0:T(8,128)(2,1)} %get-tuple-element.187), channel_id=1, source_target_pairs={{0,2},{1,3},{2,0},{3,1},{4,6},{5,7},{6,4},{7,5},{8,10},{9,11},{10,... | collective-permute-start | bytes 884744 | tf_op jit(solution)/shard_map/ppermute | solution.py:113
  401.5 6.0 %collective-permute-start.52 = (bf16[64,768]{1,0:T(8,128)(2,1)S(1)}, bf16[64,768]{1,0:T(8,128)(2,1)S(1)}, u32[]{:S(2)}, u32[]{:S(2)}) collective-permute-start(bf16[64,768]{1,0:T(8,128)(2,1)S(1)} %slice.315), channel_id=1, source_target_pairs={{0,4},{8,0},{16,8},{24,16},{28,24},{20,28},{12,20},{4,12},{1,5},{9... | collective-permute-start | bytes 294920 | tf_op jit(solution)/shard_map/ppermute | solution.py:91
  403.1 4.4 collective-permute-start.53
  408.8 5.6 %collective-permute-start.54 = (bf16[112,768]{1,0:T(8,128)(2,1)}, bf16[112,768]{1,0:T(8,128)(2,1)S(1)}, u32[]{:S(2)}, u32[]{:S(2)}) collective-permute-start(bf16[112,768]{1,0:T(8,128)(2,1)} %get-tuple-element.190), channel_id=1, source_target_pairs={{0,4},{8,0},{16,8},{24,16},{28,24},{20,28},{12,20},{4,12},{1,5},{9... | collective-permute-start | bytes 516104 | tf_op jit(solution)/shard_map/ppermute | solution.py:91
  410.3 5.6 %collective-permute-start.55 = (bf16[112,768]{1,0:T(8,128)(2,1)}, bf16[112,768]{1,0:T(8,128)(2,1)S(1)}, u32[]{:S(2)}, u32[]{:S(2)}) collective-permute-start(bf16[112,768]{1,0:T(8,128)(2,1)} %get-tuple-element.191), channel_id=1, source_target_pairs={{0,8},{8,16},{16,24},{24,28},{28,20},{20,12},{12,4},{4,0},{1,9},{9... | collective-permute-start | bytes 516104 | tf_op jit(solution)/shard_map/ppermute | solution.py:88
  410.8 9.9 %collective-permute-start.49 = (bf16[3,96,768]{2,1,0:T(8,128)(2,1)S(1)}, bf16[3,96,768]{2,1,0:T(8,128)(2,1)S(1)}, u32[]{:S(2)}, u32[]{:S(2)}) collective-permute-start(bf16[3,96,768]{2,1,0:T(8,128)(2,1)S(1)} %copy-done.68), channel_id=1, source_target_pairs={{0,2},{1,3},{2,0},{3,1},{4,6},{5,7},{6,4},{7,5},{8,10},{9,11},{10,... | collective-permute-start | bytes 1327112 | tf_op jit(solution)/shard_map/ppermute | solution.py:113
  417.1 6.7 %collective-permute-start.56 = (bf16[112,768]{1,0:T(8,128)(2,1)S(1)}, bf16[112,768]{1,0:T(8,128)(2,1)S(1)}, u32[]{:S(2)}, u32[]{:S(2)}) collective-permute-start(bf16[112,768]{1,0:T(8,128)(2,1)S(1)} %get-tuple-element.192), channel_id=1, source_target_pairs={{0,4},{8,0},{16,8},{24,16},{28,24},{20,28},{12,20},{4,12},{1,5},{9... | collective-permute-start | bytes 516104 | tf_op jit(solution)/shard_map/ppermute | solution.py:91
  418.9 7.1 %collective-permute-start.57 = (bf16[112,768]{1,0:T(8,128)(2,1)S(1)}, bf16[112,768]{1,0:T(8,128)(2,1)S(1)}, u32[]{:S(2)}, u32[]{:S(2)}) collective-permute-start(bf16[112,768]{1,0:T(8,128)(2,1)S(1)} %get-tuple-element.193), channel_id=1, source_target_pairs={{0,8},{8,16},{16,24},{24,28},{28,20},{20,12},{12,4},{4,0},{1,9},{9... | collective-permute-start | bytes 516104 | tf_op jit(solution)/shard_map/ppermute | solution.py:88
  426.7 5.5 %collective-permute-start.58 = (bf16[112,768]{1,0:T(8,128)(2,1)S(1)}, bf16[112,768]{1,0:T(8,128)(2,1)S(1)}, u32[]{:S(2)}, u32[]{:S(2)}) collective-permute-start(bf16[112,768]{1,0:T(8,128)(2,1)S(1)} %get-tuple-element.194), channel_id=1, source_target_pairs={{0,4},{8,0},{16,8},{24,16},{28,24},{20,28},{12,20},{4,12},{1,5},{9... | collective-permute-start | bytes 516104 | tf_op jit(solution)/shard_map/ppermute | solution.py:91
  427.4 5.4 %collective-permute-start.59 = (bf16[112,768]{1,0:T(8,128)(2,1)S(1)}, bf16[112,768]{1,0:T(8,128)(2,1)S(1)}, u32[]{:S(2)}, u32[]{:S(2)}) collective-permute-start(bf16[112,768]{1,0:T(8,128)(2,1)S(1)} %get-tuple-element.195), channel_id=1, source_target_pairs={{0,8},{8,16},{16,24},{24,28},{28,20},{20,12},{12,4},{4,0},{1,9},{9... | collective-permute-start | bytes 516104 | tf_op jit(solution)/shard_map/ppermute | solution.py:88
  (115 other events, 976.8 us)
Sparse Core Ops, SparseCore 0:
  73.4 65.0 all-gather.1
  294.6 80.0 reduce-scatter.1
